TPU v7x, 32 devices: a whole 2x2x4 slice. The times are simulated.
32 devices in a mesh: req: 8 (over y, x, core), tp: 4 (over z).
Axes of the slice: x: 2, y: 2, z: 4, core: 2. Of those that a mesh axis runs over, the one named last changes fastest.
Arguments:
- hidden: bfloat16 [64, 24, 2560], P('req', None, 'tp'), may hold values from -6 to 6
- norm_gain: float32 [2560], replicated, may hold values from 0.25 to 1.75
- w_query: bfloat16 [2560, 2560], P(None, 'tp'), may hold values from -0.125 to 0.125
- w_keyval: bfloat16 [1280, 2560], P('tp'), may hold values from -0.125 to 0.125
- w_out: bfloat16 [2560, 2560], P('tp'), may hold values from -0.25 to 0.25
- kv_cache: bfloat16 [64, 1280, 512], P('req', 'tp'), as said below
- lengths: int32 [64], P('req'), may hold values from 2 to 508, as said below
- parents: int32 [64, 24], P('req'), may hold values from 0 to 22, as said below
- accepted: int32 [64, 4], P('req'), may hold values from 0 to 6, as said below
- slot_of: int32 [64], P('req'), may hold values from 0 to 63, as said below
Outputs:
- out_rows: bfloat16 [64, 24, 2560], P('req', None, 'tp')
- new_cache: bfloat16 [64, 1280, 512], P('req', 'tp')
Inputs may be any that keep to these rules, and one draw needn't show every extreme that they name: `lengths`: some request has exactly 508 cached tokens. parents[r, 0] = 0 and parents[r, t] is t - 1 or max(t - 2, 0) for t >= 1. accepted[r, m] is the tree token at depth m on the path from token 0 to one token of request r, so accepted[r, 0] = 0. A permutation; the 8 requests held by req index i go to 8 different req indices, one to each: a request of index i lands in slot d * 8 + i, where d = slot_of // 8. `kv_cache`: keys and values of cached tokens; positions at or past a request's length are not read.
All inputs are finite; a program needn't handle non-finite values.
Results may differ from a plain program's by a relative error of at most 0.012.
Values may be sent and summed in bfloat16 or wider, within the bound.
A program may use at most 128 MiB of HBM per device.

v0:
```python
import math

import jax
import jax.numpy as jnp
from jax import lax
from jax.sharding import PartitionSpec as P

H = 32
KVH = 8
HD = 80


def ancestry(parents):
    tree_size = parents.shape[-1]
    tokens = jnp.arange(tree_size, dtype=jnp.int32)

    def follow(index_step, state):
        marks, depths, current = state
        marks = jnp.logical_or(marks, current[..., :, None] == tokens)
        depths = depths + (current != 0).astype(jnp.int32)
        current = jnp.take_along_axis(parents, current, axis=-1)
        return (marks, depths, current)

    start = jnp.broadcast_to(tokens, parents.shape)
    marks = jnp.zeros(parents.shape + (tree_size,), jnp.bool_)
    marks, depths, finished = lax.fori_loop(
        0, tree_size, follow, (marks, jnp.zeros(parents.shape, jnp.int32), start)
    )
    return (marks, depths)


def rope_tables(positions):
    frequency = 10000.0 ** (-2.0 * jnp.arange(HD // 2, dtype=jnp.float32) / HD)
    angles = positions.astype(jnp.float32)[..., None] * frequency
    return (jnp.cos(angles), jnp.sin(angles))


def rotate_pairs(values, cosines, sines):
    half_size = values.shape[-1] // 2
    first_half = values[..., :half_size]
    second_half = values[..., half_size:]
    return jnp.concatenate(
        [first_half * cosines - second_half * sines, second_half * cosines + first_half * sines],
        axis=-1,
    )


def place_columns(kept_rows, new_columns, start):
    return lax.dynamic_update_slice(kept_rows, new_columns, (jnp.zeros((), jnp.int32), start))


def verify_layer(rows, norm_gain, w_query, w_keyval, w_out, kv_cache, lengths, parents, accepted):
    requests, tree_size, shard_width = rows.shape
    cache_len = kv_cache.shape[2]
    group_size = H // KVH
    kv_local = w_keyval.shape[0] // (2 * HD)
    score_scale = 1.0 / math.sqrt(HD)
    full_rows = lax.all_gather(rows, "tp", axis=2, tiled=True)
    values = full_rows.astype(jnp.float32)
    spread = jnp.mean(values * values, axis=-1, keepdims=True)
    normed = (values * lax.rsqrt(spread + 1e-05) * norm_gain).astype(jnp.bfloat16)
    flat_rows = normed.reshape(requests * tree_size, -1)
    query = jnp.dot(flat_rows, w_query, preferred_element_type=jnp.float32).reshape(
        requests, tree_size, kv_local, group_size, HD
    )
    keyval = lax.dot_general(
        flat_rows, w_keyval, (((1,), (1,)), ((), ())), preferred_element_type=jnp.float32
    ).reshape(requests, tree_size, kv_local, 2, HD)
    ancestors, depths = ancestry(parents)
    cosines, sines = rope_tables(lengths[:, None] + depths)
    query = rotate_pairs(query, cosines[:, :, None, None], sines[:, :, None, None]).astype(
        jnp.bfloat16
    )
    keys = rotate_pairs(keyval[:, :, :, 0], cosines[:, :, None], sines[:, :, None]).astype(
        jnp.bfloat16
    )
    tree_values = keyval[:, :, :, 1].astype(jnp.bfloat16)
    cached = kv_cache.reshape(requests, kv_local, 2, HD, cache_len)
    cache_scores = (
        jnp.einsum("rtgqe,rgec->rgqtc", query, cached[:, :, 0], preferred_element_type=jnp.float32)
        * score_scale
    )
    tree_scores = (
        jnp.einsum("rtgqe,rsge->rgqts", query, keys, preferred_element_type=jnp.float32)
        * score_scale
    )
    positions = jnp.arange(cache_len, dtype=jnp.int32)
    live_rows = positions[None, :] < lengths[:, None]
    cache_scores = jnp.where(live_rows[:, None, None, None, :], cache_scores, -jnp.inf)
    tree_scores = jnp.where(ancestors[:, None, None, :, :], tree_scores, -jnp.inf)
    row_max = jnp.maximum(jnp.max(cache_scores, axis=-1), jnp.max(tree_scores, axis=-1))[..., None]
    cache_weights = jnp.exp(cache_scores - row_max)
    tree_weights = jnp.exp(tree_scores - row_max)
    denominator = (jnp.sum(cache_weights, axis=-1) + jnp.sum(tree_weights, axis=-1))[..., None]
    cache_probs = (cache_weights / denominator).astype(jnp.bfloat16)
    tree_probs = (tree_weights / denominator).astype(jnp.bfloat16)
    context = jnp.einsum(
        "rgqtc,rgec->rtgqe", cache_probs, cached[:, :, 1], preferred_element_type=jnp.float32
    )
    context = context + jnp.einsum(
        "rgqts,rsge->rtgqe", tree_probs, tree_values, preferred_element_type=jnp.float32
    )
    context = context.astype(jnp.bfloat16).reshape(requests * tree_size, -1)
    partial_value = jnp.dot(context, w_out, preferred_element_type=jnp.float32).reshape(
        requests, tree_size, -1
    )
    summed = lax.psum_scatter(
        partial_value.astype(jnp.bfloat16), "tp", scatter_dimension=2, tiled=True
    ).astype(jnp.float32)
    out_rows = (rows.astype(jnp.float32) + summed).astype(jnp.bfloat16)
    tree_kv = jnp.stack([keys, tree_values], axis=3).reshape(requests, tree_size, -1)
    accepted_kv = jnp.transpose(
        jnp.take_along_axis(tree_kv, accepted[:, :, None], axis=1), (0, 2, 1)
    )
    kept = jnp.where(live_rows[:, None, :], kv_cache, jnp.zeros((), jnp.bfloat16))
    compacted = jax.vmap(place_columns)(kept, accepted_kv, lengths)
    return (out_rows, compacted)


def per_device(
    hidden, norm_gain, w_query, w_keyval, w_out, kv_cache, lengths, parents, accepted, slot_of
):
    held_count = hidden.shape[0]
    destination = slot_of // held_count
    peer_index = jnp.arange(held_count, dtype=jnp.int32)
    matches = (destination[None, :] == peer_index[:, None]).astype(jnp.int32)
    send_order = jnp.sum(matches * peer_index[None, :], axis=1)
    out_rows, compacted = verify_layer(
        hidden, norm_gain, w_query, w_keyval, w_out, kv_cache, lengths, parents, accepted
    )
    new_cache = lax.all_to_all(
        jnp.take(compacted, send_order, axis=0), "req", split_axis=0, concat_axis=0, tiled=True
    )
    return (out_rows, new_cache)


def solution(mesh):
    in_specs = (
        P("req", None, "tp"),
        P(),
        P(None, "tp"),
        P("tp", None),
        P("tp", None),
        P("req", "tp", None),
        P("req"),
        P("req", None),
        P("req", None),
        P("req"),
    )
    out_specs = (P("req", None, "tp"), P("req", "tp", None))
    return jax.shard_map(
        per_device, mesh=mesh, in_specs=in_specs, out_specs=out_specs, check_vma=False
    )
```

profile of v0, /device:TPU:0, one launch (start us, length us, event | category | flops | bytes accessed | tf_op | source)
XLA Modules:
  0.0 258.2 jit_solution(6070322368242678684)
XLA Ops:
  7.2 24.0 %all_gather.3 = bf16[8,24,2560]{2,1,0:T(8,128)(2,1)S(1)} all-gather(bf16[8,24,640]{2,1,0:T(8,128)(2,1)} %param.12), channel_id=1, replica_groups=mesh['req'=8,'tp'=4] {'tp'}, dimensions={2}, use_global_device_ids=true | all-gather | bytes 1228800 | tf_op jit(solution)/shard_map/all_gather | solution.py:58
  36.1 37.0 %while.17 = (s32[]{:T(128)}, pred[8,24,24]{2,1,0:T(8,128)(4,1)S(1)}, s32[8,24]{1,0:T(8,128)S(1)}, s32[8,24]{1,0:T(8,128)S(1)}, s32[8,24]{1,0:T(8,128)S(1)}, /*index=5*/s32[]{:T(128)}, s32[]{:T(128)}) while((s32[]{:T(128)}, pred[8,24,24]{2,1,0:T(8,128)(4,1)S(1)}, s32[8,24]{1,0:T(8,128)S(1)}, s32[8,24]{1,0:T(8,128)S(1)}, ...), condition=%wide.region_2.3_spmd.clone, body=%wide.region_1.2_spmd.clone.sunk | while | flops 17475 | bytes 21592 | solution.py:26
  82.0 3.4 %broadcast_select_fusion.1 = bf16[8,320,512]{2,1,0:T(8,128)(2,1)} fusion(bf16[8,320,512]{2,1,0:T(8,128)(2,1)} %param.17, pred[8,512]{1,0:T(8,128)(4,1)S(1)} %iota_compare_fusion.1), kind=kLoop, calls=%fused_computation.21 | loop fusion | flops 1310720 | bytes 5246976 | tf_op jit(solution)/shard_map/jit(_where)/select_n | solution.py:115
  85.6 75.5 %while.16 = (s32[]{:T(128)}, bf16[8,320,512]{2,1,0:T(8,128)(2,1)}, s32[8,3]{0,1:T(4,128)S(1)}, bf16[8,320,4]{2,1,0:T(8,128)(2,1)}, s32[]{:T(128)}, /*index=5*/s32[3]{0:T(128)S(1)}, s32[]{:T(128)}) while((s32[]{:T(128)}, bf16[8,320,512]{2,1,0:T(8,128)(2,1)}, s32[8,3]{0,1:T(4,128)S(1)}, bf16[8,320,4]{2,1,0:T(8,128)(2,1)}, s32[]{:T(128)}, ...), condition=%wide.while_cond, body=%wide.while_body.sunk | while | flops 1299 | bytes 12971 | solution.py:49
  88.9 2.9 %dynamic-slice_select_fusion.2 = bf16[1,320,4]{2,1,0:T(8,128)(2,1)S(1)} fusion(bf16[8,320,4]{2,1,0:T(8,128)(2,1)} %get-tuple-element.202, s32[]{:T(128)} %get-tuple-element.192, bf16[8,320,512]{2,1,0:T(8,128)(2,1)} %get-tuple-element.193, s32[]{:T(128)} %bitcast.115, s32[]{:T(128)} %bitcast.116, pred[]{:T(512)} %and_reduce_fusion.2), kind=kLoop, calls=%fused_computation.4.clone.1 | loop fusion | flops 1280 | bytes 7693 | tf_op jit(solution)/shard_map/vmap(vmap())/scatter
  91.8 3.2 %dynamic-update-slice.3 = bf16[8,320,512]{2,1,0:T(8,128)(2,1)} dynamic-update-slice(bf16[8,320,512]{2,1,0:T(8,128)(2,1)} %get-tuple-element.193, bf16[1,320,4]{2,1,0:T(8,128)(2,1)S(1)} %dynamic-slice_select_fusion.2, s32[]{:T(128)} %bitcast.115, s32[]{:T(128)} %constant.55.clone.1..sunk, s32[]{:T(128)} %bitcast.116) | dynamic-update-slice | bytes 5124 | tf_op jit(solution)/shard_map/vmap(vmap())/scatter
  101.2 3.0 %dynamic-update-slice.3 = bf16[8,320,512]{2,1,0:T(8,128)(2,1)} dynamic-update-slice(bf16[8,320,512]{2,1,0:T(8,128)(2,1)} %get-tuple-element.193, bf16[1,320,4]{2,1,0:T(8,128)(2,1)S(1)} %dynamic-slice_select_fusion.2, s32[]{:T(128)} %bitcast.115, s32[]{:T(128)} %constant.55.clone.1..sunk, s32[]{:T(128)} %bitcast.116) | dynamic-update-slice | bytes 5124 | tf_op jit(solution)/shard_map/vmap(vmap())/scatter
  110.5 3.2 %dynamic-update-slice.3 = bf16[8,320,512]{2,1,0:T(8,128)(2,1)} dynamic-update-slice(bf16[8,320,512]{2,1,0:T(8,128)(2,1)} %get-tuple-element.193, bf16[1,320,4]{2,1,0:T(8,128)(2,1)S(1)} %dynamic-slice_select_fusion.2, s32[]{:T(128)} %bitcast.115, s32[]{:T(128)} %constant.55.clone.1..sunk, s32[]{:T(128)} %bitcast.116) | dynamic-update-slice | bytes 5124 | tf_op jit(solution)/shard_map/vmap(vmap())/scatter
  119.9 3.2 %dynamic-update-slice.3 = bf16[8,320,512]{2,1,0:T(8,128)(2,1)} dynamic-update-slice(bf16[8,320,512]{2,1,0:T(8,128)(2,1)} %get-tuple-element.193, bf16[1,320,4]{2,1,0:T(8,128)(2,1)S(1)} %dynamic-slice_select_fusion.2, s32[]{:T(128)} %bitcast.115, s32[]{:T(128)} %constant.55.clone.1..sunk, s32[]{:T(128)} %bitcast.116) | dynamic-update-slice | bytes 5124 | tf_op jit(solution)/shard_map/vmap(vmap())/scatter
  129.4 3.2 %dynamic-update-slice.3 = bf16[8,320,512]{2,1,0:T(8,128)(2,1)} dynamic-update-slice(bf16[8,320,512]{2,1,0:T(8,128)(2,1)} %get-tuple-element.193, bf16[1,320,4]{2,1,0:T(8,128)(2,1)S(1)} %dynamic-slice_select_fusion.2, s32[]{:T(128)} %bitcast.115, s32[]{:T(128)} %constant.55.clone.1..sunk, s32[]{:T(128)} %bitcast.116) | dynamic-update-slice | bytes 5124 | tf_op jit(solution)/shard_map/vmap(vmap())/scatter
  135.9 2.9 %dynamic-slice_select_fusion.2 = bf16[1,320,4]{2,1,0:T(8,128)(2,1)S(1)} fusion(bf16[8,320,4]{2,1,0:T(8,128)(2,1)} %get-tuple-element.202, s32[]{:T(128)} %get-tuple-element.192, bf16[8,320,512]{2,1,0:T(8,128)(2,1)} %get-tuple-element.193, s32[]{:T(128)} %bitcast.115, s32[]{:T(128)} %bitcast.116, pred[]{:T(512)} %and_reduce_fusion.2), kind=kLoop, calls=%fused_computation.4.clone.1 | loop fusion | flops 1280 | bytes 7693 | tf_op jit(solution)/shard_map/vmap(vmap())/scatter
  138.9 3.2 %dynamic-update-slice.3 = bf16[8,320,512]{2,1,0:T(8,128)(2,1)} dynamic-update-slice(bf16[8,320,512]{2,1,0:T(8,128)(2,1)} %get-tuple-element.193, bf16[1,320,4]{2,1,0:T(8,128)(2,1)S(1)} %dynamic-slice_select_fusion.2, s32[]{:T(128)} %bitcast.115, s32[]{:T(128)} %constant.55.clone.1..sunk, s32[]{:T(128)} %bitcast.116) | dynamic-update-slice | bytes 5124 | tf_op jit(solution)/shard_map/vmap(vmap())/scatter
  145.4 2.9 %dynamic-slice_select_fusion.2 = bf16[1,320,4]{2,1,0:T(8,128)(2,1)S(1)} fusion(bf16[8,320,4]{2,1,0:T(8,128)(2,1)} %get-tuple-element.202, s32[]{:T(128)} %get-tuple-element.192, bf16[8,320,512]{2,1,0:T(8,128)(2,1)} %get-tuple-element.193, s32[]{:T(128)} %bitcast.115, s32[]{:T(128)} %bitcast.116, pred[]{:T(512)} %and_reduce_fusion.2), kind=kLoop, calls=%fused_computation.4.clone.1 | loop fusion | flops 1280 | bytes 7693 | tf_op jit(solution)/shard_map/vmap(vmap())/scatter
  148.3 3.2 %dynamic-update-slice.3 = bf16[8,320,512]{2,1,0:T(8,128)(2,1)} dynamic-update-slice(bf16[8,320,512]{2,1,0:T(8,128)(2,1)} %get-tuple-element.193, bf16[1,320,4]{2,1,0:T(8,128)(2,1)S(1)} %dynamic-slice_select_fusion.2, s32[]{:T(128)} %bitcast.115, s32[]{:T(128)} %constant.55.clone.1..sunk, s32[]{:T(128)} %bitcast.116) | dynamic-update-slice | bytes 5124 | tf_op jit(solution)/shard_map/vmap(vmap())/scatter
  157.8 3.2 %dynamic-update-slice.3 = bf16[8,320,512]{2,1,0:T(8,128)(2,1)} dynamic-update-slice(bf16[8,320,512]{2,1,0:T(8,128)(2,1)} %get-tuple-element.193, bf16[1,320,4]{2,1,0:T(8,128)(2,1)S(1)} %dynamic-slice_select_fusion.2, s32[]{:T(128)} %bitcast.115, s32[]{:T(128)} %constant.55.clone.1..sunk, s32[]{:T(128)} %bitcast.116) | dynamic-update-slice | bytes 5124 | tf_op jit(solution)/shard_map/vmap(vmap())/scatter
  161.1 4.0 %gather_fusion.1 = bf16[8,320,512]{2,1,0:T(8,128)(2,1)} fusion(bf16[8,320,512]{2,1,0:T(8,128)(2,1)} %get-tuple-element.42, s32[1024]{0:T(1024)S(1)} %pad_clamp_fusion), kind=kCustom, calls=%fused_computation.1 | custom fusion | bytes 5242912 | tf_op jit(solution)/shard_map/jit(_take)/gather | solution.py:132
  165.0 3.5 %broadcast_select_fusion = bf16[8,320,512]{2,1,0:T(8,128)(2,1)} fusion(bf16[8,320,512]{2,1,0:T(8,128)(2,1)} %gather_fusion.1, pred[8]{0:T(512)(128)(4,1)S(1)} %copy-done.18), kind=kLoop, calls=%fused_computation.20 | loop fusion | flops 1310720 | bytes 5242888 | tf_op jit(solution)/shard_map/jit(_take)/select_n | solution.py:132
  168.6 4.4 %all-to-all-start = ((bf16[8,320,512]{2,1,0:T(8,128)(2,1)}), bf16[8,320,512]{2,1,0:T(8,128)(2,1)}, u32[]{:S(2)}, u32[]{:S(2)}) async-start(bf16[8,320,512]{2,1,0:T(8,128)(2,1)} %broadcast_select_fusion), calls=%async_computation | async-start | bytes 5242880 | tf_op jit(solution)/shard_map/all_to_all | solution.py:131
  173.2 5.7 %copy.44 = bf16[2560,640]{0,1:T(8,128)(2,1)} copy(bf16[2560,640]{1,0:T(8,128)(2,1)} %param.14) | data formatting | bytes 6553600 | tf_op args[2]
  178.9 3.6 %fusion.20 = f32[8,24,2,4,80]{4,1,3,2,0:T(8,128)S(1)} fusion(bf16[2,4,80,2560,1]{3,2,1,0,4:T(8,128)(2,1)} %bitcast.125, bf16[8,24,2560]{2,1,0:T(8,128)(2,1)} %copy-done.3, f32[2560]{0:T(1024)S(1)} %copy-done.19, f32[8,24]{1,0:T(8,128)S(1)} %add_rsqrt_fusion), kind=kOutput, calls=%fused_computation.47 | convolution fusion | flops 631111680 | bytes 4762368 | tf_op jit(solution)/shard_map/dot_general | solution.py:63
  196.4 5.8 %copy.62 = bf16[8,24,2560]{1,0,2:T(8,128)(2,1)} copy(bf16[8,24,2560]{2,1,0:T(8,128)(2,1)} %convolution_convert_fusion) | data formatting | bytes 1966080
  202.1 7.3 %reshape.231 = bf16[2560,192]{1,0:T(8,128)(2,1)} reshape(bf16[2560,8,24]{2,1,0:T(8,128)(2,1)} %bitcast.121) | data formatting | bytes 1966080
  209.4 31.3 %reduce-scatter.4.cloned.1.call-done = bf16[640,192]{1,0:T(8,128)(2,1)} async-done(((bf16[2560,192]{1,0:T(8,128)(2,1)}), bf16[640,192]{1,0:T(8,128)(2,1)}) %reduce-scatter.4.cloned.1.call-update) | async-done | bytes 245776
  248.0 3.4 %copy.87 = bf16[8,320,512]{2,1,0:T(8,128)(2,1)} copy(bf16[8,320,512]{2,1,0:T(8,128)(2,1)} %all-to-all-done) | data formatting | bytes 5242880
  (269 shorter events, 111.9 us)
Async XLA Ops:
  7.2 187.2 %copy-start = (bf16[640,2560]{1,0:T(8,128)(2,1)S(1)}, bf16[640,2560]{1,0:T(8,128)(2,1)}, u32[]{:S(2)}) copy-start(bf16[640,2560]{1,0:T(8,128)(2,1)} %param.16) | copy-start | bytes 9830404
  31.2 2.7 %copy-start.3 = (bf16[8,24,2560]{2,1,0:T(8,128)(2,1)}, bf16[8,24,2560]{2,1,0:T(8,128)(2,1)S(1)}, u32[]{:S(2)}) copy-start(bf16[8,24,2560]{2,1,0:T(8,128)(2,1)S(1)} %all_gather.3) | copy-start | bytes 2949124
  31.5 3.8 %copy-start.16 = (s32[8,4]{0,1:T(4,128)S(1)}, s32[8,4]{0,1:T(4,128)}, u32[]{:S(2)}) copy-start(s32[8,4]{0,1:T(4,128)} %param.20) | copy-start | bytes 388
  31.5 3.8 %copy-start.17 = (s32[8]{0:T(128)S(1)}, s32[8]{0:T(128)}, u32[]{:S(2)}) copy-start(s32[8]{0:T(128)} %param.18) | copy-start | bytes 100
  31.5 3.9 %copy-start.20 = (s32[8]{0:T(128)S(1)}, s32[8]{0:T(128)}, u32[]{:S(2)}) copy-start(s32[8]{0:T(128)} %param.21) | copy-start | bytes 100
  31.5 4.6 %copy-start.1 = (s32[8,24]{1,0:T(8,128)S(1)}, s32[8,24]{1,0:T(8,128)}, u32[]{:S(2)}) copy-start(s32[8,24]{1,0:T(8,128)} %param.19) | copy-start | bytes 2308
  33.9 0.8 copy-start.13
  73.7 0.6 copy-start.5
  73.7 0.7 copy-start.7
  74.3 0.6 copy-start.9
  74.3 1.6 copy-start.11
  82.0 3.5 %copy-start.15 = (s32[3]{0:T(128)S(1)}, s32[3]{0:T(128)}, u32[]{:S(2)}) copy-start(s32[3]{0:T(128)} %constant.222) | copy-start | bytes 40
  161.1 4.0 %copy-start.18 = (pred[8]{0:T(512)(128)(4,1)S(1)}, pred[8]{0:T(512)(128)(4,1)}, u32[]{:S(2)}) copy-start(pred[8]{0:T(512)(128)(4,1)} %compare_and_fusion.1) | copy-start | bytes 28
  168.6 79.4 %all-to-all-start = ((bf16[8,320,512]{2,1,0:T(8,128)(2,1)}), bf16[8,320,512]{2,1,0:T(8,128)(2,1)}, u32[]{:S(2)}, u32[]{:S(2)}) async-start(bf16[8,320,512]{2,1,0:T(8,128)(2,1)} %broadcast_select_fusion), calls=%async_computation | async-start | bytes 5242880 | tf_op jit(solution)/shard_map/all_to_all | solution.py:131
  173.0 5.9 %copy-start.19 = (f32[2560]{0:T(1024)S(1)}, f32[2560]{0:T(1024)}, u32[]{:S(2)}) copy-start(f32[2560]{0:T(1024)} %param.13) | copy-start | bytes 30724
  173.0 67.7 %reduce-scatter.4.cloned.1.call-start = ((), (), s32[]{:S(2)}) async-start(), calls=%async_computation.2 | async-start | bytes 1638400
  178.9 3.6 %copy-start.6 = (f32[8,24,40]{2,1,0:T(8,128)S(1)}, f32[8,24,40]{2,1,0:T(8,128)}, u32[]{:S(2)}) copy-start(f32[8,24,40]{2,1,0:T(8,128)} %copy-done.5) | copy-start | bytes 92164
  178.9 3.7 %copy-start.8 = (f32[8,24,40]{2,1,0:T(8,128)S(1)}, f32[8,24,40]{2,1,0:T(8,128)}, u32[]{:S(2)}) copy-start(f32[8,24,40]{2,1,0:T(8,128)} %copy-done.7) | copy-start | bytes 92164
  182.6 1.4 copy-start.10
  182.6 1.4 copy-start.12
  188.3 1.7 copy-start.2
  190.1 1.7 copy-start.14
  209.4 36.9 %copy-start.4 = (bf16[8,24,640]{2,1,0:T(8,128)(2,1)S(1)}, bf16[8,24,640]{2,1,0:T(8,128)(2,1)}, u32[]{:S(2)}) copy-start(bf16[8,24,640]{2,1,0:T(8,128)(2,1)} %param.12) | copy-start | bytes 737284
Sparse Core Ops, SparseCore 0:
  209.5 31.1 reduce-scatter.3
where the time goes:
time: 260 us; the launch traced here: 258 us
  local copies, waits for them, and re-layouts  104 us (40%)
  other arithmetic  64.1 us (25%)
  waiting for transfers between devices  31.4 us (12%)
  blocking collectives  24 us (9%)
  between operations  14.4 us (6%)
  matrix products  14.3 us (6%)
  starting transfers between devices  4.63 us (2%)
    scatter x16, other arithmetic  44.6 us
    gather x72, local copies, waits for them, and re-layouts, follow(): current = jnp.take_along_axis(parents, current, axis=-1)  32.8 us
    unnamed x2, waiting for transfers between devices  31.4 us
    scatter x24, local copies, waits for them, and re-layouts  30.8 us
    unnamed x49, local copies, waits for them, and re-layouts  29.8 us
    all_gather x1, blocking collectives, verify_layer(): full_rows = lax.all_gather(rows, 'tp', axis=2, tiled=True)  24 us
  transfers between devices with their start and end apart: 2, of which 1 were waited for; matrix products, arithmetic and copies ran while one was open for 17% of the time, Pallas kernels for 0%

commit v1 on v0

v1 whole, which is shorter than its diff:
```python
import functools
import math

import jax
import jax.numpy as jnp
import numpy as np
from jax import lax
from jax.experimental import pallas as pl
from jax.experimental.pallas import tpu as pltpu
from jax.sharding import PartitionSpec as P

H = 32
KVH = 8
HD = 80
HALF = HD // 2
GROUP = H // KVH
MESH = pl.DeviceIdType.MESH
F32 = jnp.float32
BF16 = jnp.bfloat16
PAD = 16


def kernel(
    n, t, chunks, requests, tree,
    lengths, slots, accepted, hidden, gain, freq, parent, w_query, w_keyval, w_out, cache,
    out_rows, new_cache,
    wq, wkv, wo, kept, stage, landed, note_out, note_in, full, nrm, qs, kvs, marks, depth,
    ctx, part, terms,
    w_sem, cache_sem, ag_send, ag_recv, rs_send, rs_recv, move_send, move_recv,
    note_send, note_recv, out_sem,
):
    req, tp = lax.axis_index("req"), lax.axis_index("tp")
    rows, width = hidden.shape
    per = requests // chunks
    crows = per * tree
    cache_len = cache.shape[2]
    kv_local = wkv.shape[0] // (2 * HD)
    scale = 1.0 / math.sqrt(HD)

    def at_req(k):
        return lax.rem(req + k, n)

    def at_tp(k):
        return lax.rem(tp + k, t)

    def load_cache(r, carry):
        pltpu.make_async_copy(cache.at[r], kept.at[r], cache_sem.at[r]).start()
        return carry

    lax.fori_loop(0, requests, load_cache, 0)
    loads = [
        pltpu.make_async_copy(src, dst, w_sem.at[i])
        for i, (src, dst) in enumerate(((w_query, wq), (w_keyval, wkv), (w_out, wo)))
    ]
    for copy in loads:
        copy.start()

    barrier = pltpu.get_barrier_semaphore()
    for k in range(1, n):
        pl.semaphore_signal(barrier, inc=1, device_id=(at_req(k), tp), device_id_type=MESH)
    for k in range(1, t):
        pl.semaphore_signal(barrier, inc=1, device_id=(req, at_tp(k)), device_id_type=MESH)
    pl.semaphore_wait(barrier, n + t - 2)

    def gather_copy(c, k, slot):
        return pltpu.make_async_remote_copy(
            src_ref=hidden.at[pl.ds(c * crows, crows)],
            dst_ref=full.at[c, slot],
            send_sem=ag_send.at[c, k],
            recv_sem=ag_recv.at[c, slot],
            device_id=(req, at_tp(k)),
            device_id_type=MESH,
        )

    for c in range(chunks):
        for k in range(1, t):
            gather_copy(c, k, tp).start()
        full[c, tp] = hidden[c * crows : (c + 1) * crows]

    positions = lax.broadcasted_iota(jnp.int32, (1, cache_len), 1)

    def request_for(dest):
        def look(r, found):
            return jnp.where(slots[r] // requests == dest, r, found)

        return lax.fori_loop(0, requests, look, jnp.int32(0))

    def wait_cache(r, carry):
        pltpu.make_async_copy(cache.at[r], kept.at[r], cache_sem.at[r]).wait()
        return carry

    lax.fori_loop(0, requests, wait_cache, 0)

    def move_copy(k):
        return pltpu.make_async_remote_copy(
            src_ref=stage.at[k],
            dst_ref=landed.at[k],
            send_sem=move_send.at[k],
            recv_sem=move_recv.at[k],
            device_id=(at_req(k), tp),
            device_id_type=MESH,
        )

    def move(k, carry):
        r = request_for(at_req(k))
        stage[k] = jnp.where(positions < lengths[r], kept[r], jnp.zeros((), BF16))
        move_copy(k).start()
        return carry

    lax.fori_loop(1, n, move, 0)
    own = request_for(req)
    landed[0] = jnp.where(positions < lengths[own], kept[own], jnp.zeros((), BF16))

    seen = lax.broadcasted_iota(jnp.int32, (rows, rows), 1)
    line = lax.broadcasted_iota(jnp.int32, (rows, rows), 0)
    reach = jnp.logical_or(seen == parent[...], seen == line).astype(F32).astype(BF16)
    covered = 1
    while covered < tree:
        reach = jnp.minimum(jnp.dot(reach, reach, preferred_element_type=F32), 1.0).astype(BF16)
        covered *= 2
    fold = (
        lax.rem(lax.broadcasted_iota(jnp.int32, (rows, tree), 0), tree)
        == lax.broadcasted_iota(jnp.int32, (rows, tree), 1)
    ).astype(F32).astype(BF16)
    local = jnp.dot(reach, fold, preferred_element_type=F32)
    marks[...] = local.reshape(requests, tree, tree)
    depth[...] = (jnp.sum(local, axis=1, keepdims=True) - 1.0).reshape(requests, tree, 1)

    for copy in loads:
        copy.wait()

    def reduce_copy(c, k):
        return pltpu.make_async_remote_copy(
            src_ref=part.at[c, at_tp(k)],
            dst_ref=terms.at[c, tp],
            send_sem=rs_send.at[c, k],
            recv_sem=rs_recv.at[c, tp],
            device_id=(req, at_tp(k)),
            device_id_type=MESH,
        )

    def chunk(c, carry):
        for k in range(1, t):
            peer = at_tp(k)
            gather_copy(c, k, peer).wait_recv()
        spread = jnp.zeros((crows, 1), F32)
        for g in range(t):
            value = full[c, g].astype(F32)
            spread += jnp.sum(value * value, axis=1, keepdims=True)
        inverse = lax.rsqrt(spread / (t * width) + 1e-05)
        for g in range(t):
            value = full[c, g].astype(F32)
            nrm[:, g * width : (g + 1) * width] = (value * inverse * gain[g : g + 1, :]).astype(BF16)
        normed = nrm[...]
        query = jnp.dot(normed, wq[...], preferred_element_type=F32)
        keyval = lax.dot_general(
            normed, wkv[...], (((1,), (1,)), ((), ())), preferred_element_type=F32
        )
        place = jnp.concatenate(
            [depth[c * per + i] + lengths[c * per + i].astype(F32) for i in range(per)], axis=0
        )
        angles = place * freq[...]
        cosines, sines = jnp.cos(angles), jnp.sin(angles)

        def turn(value):
            first, second = value[:, :HALF], value[:, HALF:]
            return jnp.concatenate(
                [first * cosines - second * sines, second * cosines + first * sines], axis=1
            )

        for h in range(kv_local * GROUP):
            value = turn(query[:, h * HD : (h + 1) * HD])
            qs[h] = value.reshape(per, tree, HD)
        for i in range(2 * kv_local):
            value = keyval[:, i * HD : (i + 1) * HD]
            if i % 2 == 0:
                value = turn(value)
            value = value.astype(BF16).astype(F32).reshape(per, tree, HD)
            kvs[pl.ds(c * per, per), i] = value

        def attend(i, inner):
            r = c * per + i
            live = positions < lengths[r]
            mask = marks[r] > 0.5
            mask = jnp.concatenate([mask.astype(F32)] * GROUP, axis=0) > 0.5
            for g in range(kv_local):
                q = qs[g * GROUP : (g + 1) * GROUP, i].reshape(GROUP * tree, HD).astype(BF16)
                low = g * 2 * HD
                keys = kept[r, low : low + HD, :]
                values = kept[r, low + HD : low + 2 * HD, :]
                tree_keys = kvs[r, 2 * g].astype(BF16)
                tree_values = kvs[r, 2 * g + 1].astype(BF16)
                a = jnp.dot(q, keys, preferred_element_type=F32) * scale
                b = lax.dot_general(
                    q, tree_keys, (((1,), (1,)), ((), ())), preferred_element_type=F32
                ) * scale
                a = jnp.where(live, a, -1e30)
                b = jnp.where(mask, b, -1e30)
                top = jnp.maximum(
                    jnp.max(a, axis=1, keepdims=True), jnp.max(b, axis=1, keepdims=True)
                )
                a, b = jnp.exp(a - top), jnp.exp(b - top)
                total = jnp.sum(a, axis=1, keepdims=True) + jnp.sum(b, axis=1, keepdims=True)
                inverse_total = 1.0 / total
                a = (a * inverse_total).astype(BF16)
                b = (b * inverse_total).astype(BF16)
                value = lax.dot_general(
                    a, values, (((1,), (1,)), ((), ())), preferred_element_type=F32
                ) + jnp.dot(b, tree_values, preferred_element_type=F32)
                for j in range(GROUP):
                    h = g * GROUP + j
                    ctx[i, :, h * HD : (h + 1) * HD] = value[j * tree : (j + 1) * tree]
            return inner

        lax.fori_loop(0, per, attend, 0)
        rounded = ctx[...].reshape(crows, kv_local * GROUP * HD).astype(BF16)
        for g in range(t):
            part[c, g] = jnp.dot(
                rounded, wo[:, g * width : (g + 1) * width], preferred_element_type=F32
            ).astype(BF16)
        for k in range(1, t):
            reduce_copy(c, k).start()
        terms[c, tp] = part[c, tp]
        return carry

    lax.fori_loop(0, chunks, chunk, 0)

    level = lax.broadcasted_iota(jnp.int32, (PAD, tree), 0)
    token = lax.broadcasted_iota(jnp.int32, (PAD, tree), 1)
    level_c = lax.broadcasted_iota(jnp.int32, (PAD, cache_len), 0)
    place_c = lax.broadcasted_iota(jnp.int32, (PAD, cache_len), 1)
    n_accept = accepted.shape[1]

    def write_note(k, target):
        r = request_for(at_req(k))
        pick = jnp.zeros((PAD, tree), F32)
        for m in range(n_accept):
            hit = jnp.logical_and(level == m, token == accepted[r, m])
            pick = jnp.where(hit, 1.0, pick)
        pick = pick.astype(BF16)
        spot = jnp.logical_and(place_c == level_c + lengths[r], level_c < n_accept)
        target[k, 0:PAD, :] = spot.astype(F32).astype(BF16)
        chosen = [
            jnp.dot(pick, kvs[r, i].astype(BF16), preferred_element_type=F32)
            for i in range(2 * kv_local)
        ]
        chosen = jnp.concatenate(chosen, axis=1).astype(BF16)
        target[k, PAD : 2 * PAD, 0 : 2 * kv_local * HD] = chosen

    def note_copy(k):
        return pltpu.make_async_remote_copy(
            src_ref=note_out.at[k],
            dst_ref=note_in.at[k],
            send_sem=note_send.at[k],
            recv_sem=note_recv.at[k],
            device_id=(at_req(k), tp),
            device_id_type=MESH,
        )

    def send_note(k, carry):
        write_note(k, note_out)
        note_copy(k).start()
        return carry

    note_out[...] = jnp.zeros_like(note_out)
    lax.fori_loop(1, n, send_note, 0)
    note_in[0] = jnp.zeros_like(note_in[0])
    write_note(0, note_in)

    def out_copy(k):
        return pltpu.make_async_copy(
            landed.at[k], new_cache.at[lax.rem(req + n - k, n)], out_sem.at[k]
        )

    def finish(k):
        spot = note_in[k, 0:PAD, :]
        chosen = note_in[k, PAD : 2 * PAD, 0 : 2 * kv_local * HD]
        added = lax.dot_general(chosen, spot, (((0,), (0,)), ((), ())), preferred_element_type=F32)
        landed[k] = landed[k] + added.astype(BF16)
        out_copy(k).start()

    finish(0)

    def receive(k, carry):
        move_copy(k).wait_recv()
        note_copy(k).wait_recv()
        finish(k)
        return carry

    lax.fori_loop(1, n, receive, 0)

    def close(c, carry):
        for k in range(1, t):
            peer = at_tp(k)
            pltpu.make_async_remote_copy(
                src_ref=part.at[c, peer],
                dst_ref=terms.at[c, peer],
                send_sem=rs_send.at[c, k],
                recv_sem=rs_recv.at[c, peer],
                device_id=(req, peer),
                device_id_type=MESH,
            ).wait_recv()
        summed = terms[c, 0].astype(F32)
        for g in range(1, t):
            summed += terms[c, g].astype(F32)
        where = pl.ds(pl.multiple_of(c * crows, 16), crows)
        out_rows[where, :] = (hidden[where, :].astype(F32) + summed).astype(BF16)
        return carry

    lax.fori_loop(0, chunks, close, 0)

    for c in range(chunks):
        for k in range(1, t):
            gather_copy(c, k, tp).wait_send()
            reduce_copy(c, k).wait_send()

    def drain(k, carry):
        move_copy(k).wait_send()
        note_copy(k).wait_send()
        out_copy(k).wait()
        return carry

    lax.fori_loop(1, n, drain, 0)
    out_copy(0).wait()


def per_device(
    n, t,
    hidden, norm_gain, w_query, w_keyval, w_out, kv_cache, lengths, parents, accepted, slot_of
):
    requests, tree, width = hidden.shape
    rows = requests * tree
    features = w_query.shape[0]
    q_width = w_query.shape[1]
    kv_rows = w_keyval.shape[0]
    cache_len = kv_cache.shape[2]
    chunks = 2
    per = requests // chunks
    crows = per * tree
    heads = q_width // HD
    freq = jnp.asarray(
        (10000.0 ** (-2.0 * np.arange(HALF, dtype=np.float64) / HD)).astype(np.float32)
    ).reshape(1, HALF)
    parent = (parents + tree * jnp.arange(requests, dtype=jnp.int32)[:, None]).reshape(rows, 1)
    smem = pl.BlockSpec(memory_space=pltpu.SMEM)
    vmem = pl.BlockSpec(memory_space=pltpu.VMEM)
    hbm = pl.BlockSpec(memory_space=pl.ANY)
    dma = pltpu.SemaphoreType.DMA
    out_rows, new_cache = pl.pallas_call(
        functools.partial(kernel, n, t, chunks, requests, tree),
        out_shape=(
            jax.ShapeDtypeStruct((rows, width), BF16),
            jax.ShapeDtypeStruct(kv_cache.shape, BF16),
        ),
        in_specs=[smem] * 3 + [vmem] * 4 + [hbm] * 4,
        out_specs=(vmem, hbm),
        scratch_shapes=[
            pltpu.VMEM(w_query.shape, BF16),
            pltpu.VMEM(w_keyval.shape, BF16),
            pltpu.VMEM(w_out.shape, BF16),
            pltpu.VMEM(kv_cache.shape, BF16),
            pltpu.VMEM((n,) + kv_cache.shape[1:], BF16),
            pltpu.VMEM((n,) + kv_cache.shape[1:], BF16),
            pltpu.VMEM((n, 2 * PAD, cache_len), BF16),
            pltpu.VMEM((n, 2 * PAD, cache_len), BF16),
            pltpu.VMEM((chunks, t, crows, width), BF16),
            pltpu.VMEM((crows, features), BF16),
            pltpu.VMEM((heads, per, tree, HD), F32),
            pltpu.VMEM((requests, kv_rows // HD, tree, HD), F32),
            pltpu.VMEM((requests, tree, tree), F32),
            pltpu.VMEM((requests, tree, 1), F32),
            pltpu.VMEM((per, tree, q_width), F32),
            pltpu.VMEM((chunks, t, crows, width), BF16),
            pltpu.VMEM((chunks, t, crows, width), BF16),
            dma((3,)),
            dma((requests,)),
            dma((chunks, t)),
            dma((chunks, t)),
            dma((chunks, t)),
            dma((chunks, t)),
            dma((n,)),
            dma((n,)),
            dma((n,)),
            dma((n,)),
            dma((n,)),
        ],
        compiler_params=pltpu.CompilerParams(
            collective_id=0, has_side_effects=True, vmem_limit_bytes=56 * 1024 * 1024
        ),
    )(
        lengths, slot_of, accepted, hidden.reshape(rows, width), norm_gain.reshape(t, width),
        freq, parent, w_query, w_keyval, w_out, kv_cache,
    )
    return (out_rows.reshape(requests, tree, width), new_cache)


def solution(mesh):
    in_specs = (
        P("req", None, "tp"),
        P(),
        P(None, "tp"),
        P("tp", None),
        P("tp", None),
        P("req", "tp", None),
        P("req"),
        P("req", None),
        P("req", None),
        P("req"),
    )
    out_specs = (P("req", None, "tp"), P("req", "tp", None))
    return jax.shard_map(
        functools.partial(per_device, mesh.shape["req"], mesh.shape["tp"]),
        mesh=mesh, in_specs=in_specs, out_specs=out_specs, check_vma=False,
    )
```

time: 260 us -> 60.2 us (0.23)
  local copies, waits for them, and re-layouts: 104 us -> 8.45 us
  other arithmetic: 64.1 us -> 0.76 us
  Pallas kernels: 0 us -> 49.5 us
  waiting for transfers between devices: 31.4 us -> 0 us
  blocking collectives: 24 us -> 0 us
  matrix products: 14.3 us -> 0 us
  between operations: 14.4 us -> 0.65 us
  starting transfers between devices: 4.63 us -> 0 us
    pallas_call x0 -> x1, Pallas kernels: none -> 49.5 us  [per_device(): pl.pallas_call(functools.partial(kernel, n, t, chunks, requests, tree), o...]
    scatter x17 -> x0, other arithmetic: 44.6 us -> none
    gather x78 -> x0, local copies, waits for them, and re-layouts: 38.8 us -> none  [the longest x72 32.8 us: follow(): current = jnp.take_along_axis(parents, current, axis=-1)]
    unnamed x2 -> x0, waiting for transfers between devices: 31.4 us -> none
    scatter x24 -> x0, local copies, waits for them, and re-layouts: 30.8 us -> none
    all_gather x1 -> x0, blocking collectives: 24 us -> none  [verify_layer(): full_rows = lax.all_gather(rows, 'tp', axis=2, tiled=True)]
    unnamed x49 -> x3, local copies, waits for them, and re-layouts: 29.8 us -> 6.4 us
    dot_general x7 -> x0, matrix products: 14.3 us -> none  [the longest x1 3.63 us: verify_layer(): jnp.dot(flat_rows, w_query, preferred_element_type=jnp.float32)]
  transfers between devices with their start and end apart: 2 -> 0, of which waited for: 1 -> 0; matrix products, arithmetic and copies ran while one was open for 17% -> 0% of each run, Pallas kernels for 0% -> 0%
where the time goes in v1:
time: 60.2 us; the launch traced here: 59.4 us
  Pallas kernels  49.5 us (82%)
  local copies, waits for them, and re-layouts  8.45 us (14%)
  other arithmetic  0.76 us (1%)
  between operations  0.65 us (1%)
    pallas_call x1, Pallas kernels, per_device(): pl.pallas_call(functools.partial(kernel, n, t, chunks, requests, tree), o...  49.5 us
    unnamed x3, local copies, waits for them, and re-layouts  6.4 us
    reshape x1, local copies, waits for them, and re-layouts, per_device(): norm_gain.reshape(t, width)  1.31 us

profile of v1, /device:TPU:0, one launch (start us, length us, event | category | flops | bytes accessed | tf_op | source)
XLA Modules:
  0.0 59.4 jit_solution(16001795030216135154)
XLA Ops:
  0.6 0.8 %broadcast_add_fusion = s32[8,24]{1,0:T(8,128)S(1)} fusion(s32[8,24]{1,0:T(8,128)} %param.18, s32[8]{0:T(128)S(1)} %iota_multiply_fusion), kind=kLoop, calls=%fused_computation | loop fusion | flops 192 | bytes 1568 | tf_op jit(solution)/shard_map/add | solution.py:344
  1.4 1.3 %copy.14.accepted = s32[8,4]{1,0:T(8,128)} copy(s32[8,4]{0,1:T(4,128)} %param.19) | data formatting | bytes 256 | tf_op args[8]
  2.7 1.3 %reshape.25.gain = f32[4,640]{1,0:T(4,128)} reshape(f32[2560]{0:T(1024)} %param.12) | data formatting | bytes 20480 | tf_op jit(solution)/shard_map/reshape | solution.py:391
  4.1 0.7 %reshape.29.parent = s32[192,1]{1,0:T(8,128)} reshape(s32[8,24]{1,0:T(8,128)S(1)} %broadcast_add_fusion) | data formatting | bytes 1536 | tf_op jit(solution)/shard_map/reshape | solution.py:344
  4.8 49.5 %shard_map.122 = (bf16[192,640]{1,0:T(8,128)(2,1)}, bf16[8,320,512]{2,1,0:T(8,128)(2,1)}) custom-call(s32[8]{0:T(128)} %lengths.1, s32[8]{0:T(128)} %slots.1, s32[8,4]{1,0:T(8,128)} %copy.14.accepted, bf16[192,640]{1,0:T(8,128)(2,1)} %bitcast.2, f32[4,640]{1,0:T(4,128)} %reshape.25.gain, f32[1,40]{1,0:T(1,128)} %constant.5.freq, s32[192,1]{1,0:T(8,128)} %reshape.29.parent, ...), custom_call_target="tpu_custom_call" | custom-call | tf_op jit(solution)/shard_map/pallas_call | solution.py:349
  54.3 1.7 %copy.18 = bf16[8,24,640]{2,1,0:T(8,128)(2,1)} copy(bf16[8,24,640]{2,1,0:T(8,128)(2,1)} %bitcast.3) | data formatting | bytes 491520
  56.0 3.4 %copy.19 = bf16[8,320,512]{2,1,0:T(8,128)(2,1)} copy(bf16[8,320,512]{2,1,0:T(8,128)(2,1)} %get-tuple-element.9) | data formatting | bytes 5242880
  (1 shorter events, 0.0 us)

commit v2 on v1

--- a/solution.py
+++ b/solution.py
@@ -25,7 +25,7 @@
     lengths, slots, accepted, hidden, gain, freq, parent, w_query, w_keyval, w_out, cache,
     out_rows, new_cache,
     wq, wkv, wo, kept, stage, landed, note_out, note_in, full, nrm, qs, kvs, marks, depth,
-    ctx, part, terms,
+    ctx, part, outgoing, incoming, total,
     w_sem, cache_sem, ag_send, ag_recv, rs_send, rs_recv, move_send, move_recv,
     note_send, note_recv, out_sem,
 ):
@@ -58,24 +58,61 @@
     barrier = pltpu.get_barrier_semaphore()
     for k in range(1, n):
         pl.semaphore_signal(barrier, inc=1, device_id=(at_req(k), tp), device_id_type=MESH)
-    for k in range(1, t):
-        pl.semaphore_signal(barrier, inc=1, device_id=(req, at_tp(k)), device_id_type=MESH)
-    pl.semaphore_wait(barrier, n + t - 2)
-
-    def gather_copy(c, k, slot):
+
+    @pl.when(tp > 0)
+    def _():
+        pl.semaphore_signal(barrier, inc=1, device_id=(req, tp - 1), device_id_type=MESH)
+
+    @pl.when(tp < t - 1)
+    def _():
+        pl.semaphore_signal(barrier, inc=1, device_id=(req, tp + 1), device_id_type=MESH)
+
+    neighbours = (tp > 0).astype(jnp.int32) + (tp < t - 1).astype(jnp.int32)
+    pl.semaphore_wait(barrier, n - 1 + neighbours)
+
+    def ends(up):
+        behind = tp if up else t - 1 - tp
+        return behind, behind < t - 1, 1 if up else -1
+
+    def gather_copy(c, s, up, arriving=False):
+        behind, more, ahead = ends(up)
+        slot = tp - ahead * (s + 1) if arriving else tp - ahead * s
+        peer = tp - ahead if arriving else tp + ahead
+        way = 0 if up else 1
         return pltpu.make_async_remote_copy(
-            src_ref=hidden.at[pl.ds(c * crows, crows)],
+            src_ref=full.at[c, slot],
             dst_ref=full.at[c, slot],
-            send_sem=ag_send.at[c, k],
-            recv_sem=ag_recv.at[c, slot],
-            device_id=(req, at_tp(k)),
+            send_sem=ag_send.at[way, c, s],
+            recv_sem=ag_recv.at[way, c, s],
+            device_id=(req, peer),
             device_id_type=MESH,
         )
 
-    for c in range(chunks):
-        for k in range(1, t):
-            gather_copy(c, k, tp).start()
+    def gather_start(c):
         full[c, tp] = hidden[c * crows : (c + 1) * crows]
+        for up in (True, False):
+            behind, more, ahead = ends(up)
+
+            @pl.when(more)
+            def _():
+                gather_copy(c, 0, up).start()
+
+    def gather_step(c, s):
+        for up in (True, False):
+            behind, more, ahead = ends(up)
+
+            @pl.when(behind >= s)
+            def _():
+                gather_copy(c, s - 1, up, arriving=True).wait_recv()
+
+            if s < t - 1:
+
+                @pl.when(jnp.logical_and(behind >= s, more))
+                def _():
+                    gather_copy(c, s, up).start()
+
+    gather_start(0)
+    gains = gain[...].reshape(1, t * width)
 
     positions = lax.broadcasted_iota(jnp.int32, (1, cache_len), 1)
 
@@ -111,9 +148,17 @@
     own = request_for(req)
     landed[0] = jnp.where(positions < lengths[own], kept[own], jnp.zeros((), BF16))
 
-    seen = lax.broadcasted_iota(jnp.int32, (rows, rows), 1)
-    line = lax.broadcasted_iota(jnp.int32, (rows, rows), 0)
-    reach = jnp.logical_or(seen == parent[...], seen == line).astype(F32).astype(BF16)
+    if t > 1:
+        gather_step(0, 1)
+    if chunks > 1:
+        gather_start(1)
+
+    seen = lax.broadcasted_iota(jnp.int32, (rows, rows), 0)
+    line = lax.broadcasted_iota(jnp.int32, (rows, rows), 1)
+    parent_row = jnp.concatenate(
+        [parent[r : r + 1, :] + r * tree for r in range(requests)], axis=1
+    )
+    reach = jnp.logical_or(seen == parent_row, seen == line).astype(F32).astype(BF16)
     covered = 1
     while covered < tree:
         reach = jnp.minimum(jnp.dot(reach, reach, preferred_element_type=F32), 1.0).astype(BF16)
@@ -122,27 +167,62 @@
         lax.rem(lax.broadcasted_iota(jnp.int32, (rows, tree), 0), tree)
         == lax.broadcasted_iota(jnp.int32, (rows, tree), 1)
     ).astype(F32).astype(BF16)
-    local = jnp.dot(reach, fold, preferred_element_type=F32)
+    local = lax.dot_general(reach, fold, (((0,), (0,)), ((), ())), preferred_element_type=F32)
     marks[...] = local.reshape(requests, tree, tree)
     depth[...] = (jnp.sum(local, axis=1, keepdims=True) - 1.0).reshape(requests, tree, 1)
 
+    for s in range(2, t):
+        gather_step(0, s)
+
     for copy in loads:
         copy.wait()
 
-    def reduce_copy(c, k):
+    def reduce_copy(c, g, up, arriving=False):
+        behind, more, ahead = ends(up)
+        way = 0 if up else 1
         return pltpu.make_async_remote_copy(
-            src_ref=part.at[c, at_tp(k)],
-            dst_ref=terms.at[c, tp],
-            send_sem=rs_send.at[c, k],
-            recv_sem=rs_recv.at[c, tp],
-            device_id=(req, at_tp(k)),
+            src_ref=outgoing.at[c, g],
+            dst_ref=incoming.at[way, c, g],
+            send_sem=rs_send.at[c, g],
+            recv_sem=rs_recv.at[way, c, g],
+            device_id=(req, tp - ahead if arriving else tp + ahead),
             device_id_type=MESH,
         )
 
-    def chunk(c, carry):
-        for k in range(1, t):
-            peer = at_tp(k)
-            gather_copy(c, k, peer).wait_recv()
+    def reduce_step(c, q):
+        for up in (True, False):
+            behind, more, ahead = ends(up)
+            g = t - 1 - q if up else q
+            way = 0 if up else 1
+            mine = g > tp if up else g < tp
+
+            @pl.when(jnp.logical_and(mine, behind == 0))
+            def _():
+                outgoing[c, g] = part[c, g]
+                reduce_copy(c, g, up).start()
+
+            @pl.when(jnp.logical_and(mine, behind > 0))
+            def _():
+                reduce_copy(c, g, up, arriving=True).wait_recv()
+                outgoing[c, g] = (
+                    part[c, g].astype(F32) + incoming[way, c, g].astype(F32)
+                ).astype(BF16)
+                reduce_copy(c, g, up).start()
+
+    def spread_steps(action, c, first, last, third):
+        steps = list(range(first, last))
+        for s in steps[len(steps) * third // 3 : len(steps) * (third + 1) // 3]:
+            action(c, s)
+
+    def pump(c, third):
+        if c + 1 < chunks:
+            spread_steps(gather_step, c + 1, 1, t, third)
+        if c > 0:
+            spread_steps(reduce_step, c - 1, 0, t - 1, third)
+
+    def chunk(c):
+        if 0 < c < chunks - 1:
+            gather_start(c + 1)
         spread = jnp.zeros((crows, 1), F32)
         for g in range(t):
             value = full[c, g].astype(F32)
@@ -150,7 +230,7 @@
         inverse = lax.rsqrt(spread / (t * width) + 1e-05)
         for g in range(t):
             value = full[c, g].astype(F32)
-            nrm[:, g * width : (g + 1) * width] = (value * inverse * gain[g : g + 1, :]).astype(BF16)
+            nrm[:, g * width : (g + 1) * width] = (value * inverse * gains[:, g * width : (g + 1) * width]).astype(BF16)
         normed = nrm[...]
         query = jnp.dot(normed, wq[...], preferred_element_type=F32)
         keyval = lax.dot_general(
@@ -161,6 +241,8 @@
         )
         angles = place * freq[...]
         cosines, sines = jnp.cos(angles), jnp.sin(angles)
+
+        pump(c, 0)
 
         def turn(value):
             first, second = value[:, :HALF], value[:, HALF:]
@@ -212,32 +294,31 @@
                     ctx[i, :, h * HD : (h + 1) * HD] = value[j * tree : (j + 1) * tree]
             return inner
 
-        lax.fori_loop(0, per, attend, 0)
+        lax.fori_loop(0, per // 2, attend, 0)
+        pump(c, 1)
+        lax.fori_loop(per // 2, per, attend, 0)
+        pump(c, 2)
         rounded = ctx[...].reshape(crows, kv_local * GROUP * HD).astype(BF16)
         for g in range(t):
             part[c, g] = jnp.dot(
                 rounded, wo[:, g * width : (g + 1) * width], preferred_element_type=F32
             ).astype(BF16)
-        for k in range(1, t):
-            reduce_copy(c, k).start()
-        terms[c, tp] = part[c, tp]
-        return carry
-
-    lax.fori_loop(0, chunks, chunk, 0)
-
-    level = lax.broadcasted_iota(jnp.int32, (PAD, tree), 0)
-    token = lax.broadcasted_iota(jnp.int32, (PAD, tree), 1)
+
+    for c in range(chunks):
+        chunk(c)
+    reduce_step(chunks - 1, 0)
+
     level_c = lax.broadcasted_iota(jnp.int32, (PAD, cache_len), 0)
     place_c = lax.broadcasted_iota(jnp.int32, (PAD, cache_len), 1)
-    n_accept = accepted.shape[1]
+    n_accept = accepted.shape[0]
+    token = lax.broadcasted_iota(jnp.int32, (n_accept, tree), 1)
+    asked = lax.broadcasted_iota(jnp.int32, accepted.shape, 1)
 
     def write_note(k, target):
         r = request_for(at_req(k))
-        pick = jnp.zeros((PAD, tree), F32)
-        for m in range(n_accept):
-            hit = jnp.logical_and(level == m, token == accepted[r, m])
-            pick = jnp.where(hit, 1.0, pick)
-        pick = pick.astype(BF16)
+        path = jnp.sum(jnp.where(asked == r, accepted[...], 0), axis=1, keepdims=True)
+        pick = (token == path).astype(F32)
+        pick = jnp.concatenate([pick, jnp.zeros((PAD - n_accept, tree), F32)], axis=0).astype(BF16)
         spot = jnp.logical_and(place_c == level_c + lengths[r], level_c < n_accept)
         target[k, 0:PAD, :] = spot.astype(F32).astype(BF16)
         chosen = [
@@ -280,6 +361,8 @@
         out_copy(k).start()
 
     finish(0)
+    for q in range(1, t - 1):
+        reduce_step(chunks - 1, q)
 
     def receive(k, carry):
         move_copy(k).wait_recv()
@@ -290,29 +373,39 @@
     lax.fori_loop(1, n, receive, 0)
 
     def close(c, carry):
-        for k in range(1, t):
-            peer = at_tp(k)
-            pltpu.make_async_remote_copy(
-                src_ref=part.at[c, peer],
-                dst_ref=terms.at[c, peer],
-                send_sem=rs_send.at[c, k],
-                recv_sem=rs_recv.at[c, peer],
-                device_id=(req, peer),
-                device_id_type=MESH,
-            ).wait_recv()
-        summed = terms[c, 0].astype(F32)
-        for g in range(1, t):
-            summed += terms[c, g].astype(F32)
         where = pl.ds(pl.multiple_of(c * crows, 16), crows)
-        out_rows[where, :] = (hidden[where, :].astype(F32) + summed).astype(BF16)
+        total[...] = part[c, tp].astype(F32) + hidden[where, :].astype(F32)
+        for up in (True, False):
+            behind, more, ahead = ends(up)
+
+            @pl.when(behind > 0)
+            def _():
+                reduce_copy(c, tp, up, arriving=True).wait_recv()
+                total[...] += incoming[0 if up else 1, c, tp].astype(F32)
+
+        out_rows[where, :] = total[...].astype(BF16)
         return carry
 
     lax.fori_loop(0, chunks, close, 0)
 
     for c in range(chunks):
-        for k in range(1, t):
-            gather_copy(c, k, tp).wait_send()
-            reduce_copy(c, k).wait_send()
+        for up in (True, False):
+            behind, more, ahead = ends(up)
+            for s in range(t - 1):
+
+                @pl.when(jnp.logical_and(behind >= s, more))
+                def _():
+                    gather_copy(c, s, up).wait_send()
+
+        for g in range(t):
+
+            @pl.when(g > tp)
+            def _():
+                reduce_copy(c, g, True).wait_send()
+
+            @pl.when(g < tp)
+            def _():
+                reduce_copy(c, g, False).wait_send()
 
     def drain(k, carry):
         move_copy(k).wait_send()
@@ -322,6 +415,16 @@
 
     lax.fori_loop(1, n, drain, 0)
     out_copy(0).wait()
+
+
+def hand_over(rows, cache, out_rows, new_cache, sem):
+    count = cache.shape[0]
+    copies = [pltpu.make_async_copy(cache.at[i], new_cache.at[i], sem.at[i]) for i in range(count)]
+    copies.append(pltpu.make_async_copy(rows, out_rows, sem.at[count]))
+    for copy in copies:
+        copy.start()
+    for copy in copies:
+        copy.wait()
 
 
 def per_device(
@@ -341,7 +444,6 @@
     freq = jnp.asarray(
         (10000.0 ** (-2.0 * np.arange(HALF, dtype=np.float64) / HD)).astype(np.float32)
     ).reshape(1, HALF)
-    parent = (parents + tree * jnp.arange(requests, dtype=jnp.int32)[:, None]).reshape(rows, 1)
     smem = pl.BlockSpec(memory_space=pltpu.SMEM)
     vmem = pl.BlockSpec(memory_space=pltpu.VMEM)
     hbm = pl.BlockSpec(memory_space=pl.ANY)
@@ -352,7 +454,7 @@
             jax.ShapeDtypeStruct((rows, width), BF16),
             jax.ShapeDtypeStruct(kv_cache.shape, BF16),
         ),
-        in_specs=[smem] * 3 + [vmem] * 4 + [hbm] * 4,
+        in_specs=[smem] * 2 + [vmem] * 5 + [hbm] * 4,
         out_specs=(vmem, hbm),
         scratch_shapes=[
             pltpu.VMEM(w_query.shape, BF16),
@@ -372,12 +474,14 @@
             pltpu.VMEM((per, tree, q_width), F32),
             pltpu.VMEM((chunks, t, crows, width), BF16),
             pltpu.VMEM((chunks, t, crows, width), BF16),
+            pltpu.VMEM((2, chunks, t, crows, width), BF16),
+            pltpu.VMEM((crows, width), F32),
             dma((3,)),
             dma((requests,)),
+            dma((2, chunks, t)),
+            dma((2, chunks, t)),
             dma((chunks, t)),
-            dma((chunks, t)),
-            dma((chunks, t)),
-            dma((chunks, t)),
+            dma((2, chunks, t)),
             dma((n,)),
             dma((n,)),
             dma((n,)),
@@ -388,9 +492,21 @@
             collective_id=0, has_side_effects=True, vmem_limit_bytes=56 * 1024 * 1024
         ),
     )(
-        lengths, slot_of, accepted, hidden.reshape(rows, width), norm_gain.reshape(t, width),
-        freq, parent, w_query, w_keyval, w_out, kv_cache,
+        lengths, slot_of, accepted.T, hidden.reshape(rows, width), norm_gain,
+        freq, parents, w_query, w_keyval, w_out, kv_cache,
     )
+    rows_shape, cache_shape = out_rows.shape, new_cache.shape
+    out_rows, new_cache = pl.pallas_call(
+        hand_over,
+        out_shape=(
+            jax.ShapeDtypeStruct(rows_shape, BF16),
+            jax.ShapeDtypeStruct(cache_shape, BF16),
+        ),
+        in_specs=[hbm, hbm],
+        out_specs=(hbm, hbm),
+        scratch_shapes=[dma((cache_shape[0] + 1,))],
+        compiler_params=pltpu.CompilerParams(vmem_limit_bytes=60 * 1024 * 1024),
+    )(out_rows, new_cache)
     return (out_rows.reshape(requests, tree, width), new_cache)
 
 

time: 60.2 us -> 153 us (2.54)
  Pallas kernels: 49.5 us -> 152 us
  local copies, waits for them, and re-layouts: 8.45 us -> 0 us
    pallas_call x0 -> x1, Pallas kernels: none -> 88 us  [per_device(): pl.pallas_call(hand_over, out_shape=(jax.ShapeDtypeStruct(rows_shape, BF1...]
    pallas_call x1, Pallas kernels: 49.5 us -> 63.5 us  [per_device(): pl.pallas_call(functools.partial(kernel, n, t, chunks, requests, tree), o...]
    unnamed x3 -> x0, local copies, waits for them, and re-layouts: 6.4 us -> none
    reshape x2 -> x0, local copies, waits for them, and re-layouts: 2.05 us -> none  [the longest x1 1.31 us: per_device(): norm_gain.reshape(t, width)]
where the time goes in v2:
time: 153 us; the launch traced here: 152 us
  Pallas kernels  152 us (99%)
    pallas_call x1, Pallas kernels, per_device(): pl.pallas_call(hand_over, out_shape=(jax.ShapeDtypeStruct(rows_shape, BF1...  88 us
    pallas_call x1, Pallas kernels, per_device(): pl.pallas_call(functools.partial(kernel, n, t, chunks, requests, tree), o...  63.5 us

profile of v2, /device:TPU:0, one launch (start us, length us, event | category | flops | bytes accessed | tf_op | source)
XLA Modules:
  0.0 152.2 jit_solution(106857664799776917)
XLA Ops:
  0.6 63.5 %shard_map.122 = (bf16[192,640]{1,0:T(8,128)(2,1)}, bf16[8,320,512]{2,1,0:T(8,128)(2,1)}) custom-call(s32[8]{0:T(128)} %lengths.1, s32[8]{0:T(128)} %slots.1, s32[4,8]{1,0:T(4,128)} %bitcast.4, bf16[192,640]{1,0:T(8,128)(2,1)} %bitcast.3, f32[2560]{0:T(1024)} %gain.1, f32[1,40]{1,0:T(1,128)} %constant.3.freq, s32[8,24]{1,0:T(8,128)} %parent.1, ...), custom_call_target="tpu_custom_call" | custom-call | tf_op jit(solution)/shard_map/pallas_call | solution.py:451
  64.2 88.0 %shard_map.123 = (bf16[192,640]{1,0:T(8,128)(2,1)}, bf16[8,320,512]{2,1,0:T(8,128)(2,1)}) custom-call(bf16[192,640]{1,0:T(8,128)(2,1)} %get-tuple-element.6.rows, bf16[8,320,512]{2,1,0:T(8,128)(2,1)} %get-tuple-element.7.cache), custom_call_target="tpu_custom_call" | custom-call | tf_op jit(solution)/shard_map/pallas_call | solution.py:499

commit v3 on v1

--- a/solution.py
+++ b/solution.py
@@ -25,7 +25,7 @@
     lengths, slots, accepted, hidden, gain, freq, parent, w_query, w_keyval, w_out, cache,
     out_rows, new_cache,
     wq, wkv, wo, kept, stage, landed, note_out, note_in, full, nrm, qs, kvs, marks, depth,
-    ctx, part, terms,
+    ctx, part, outgoing, incoming, turns,
     w_sem, cache_sem, ag_send, ag_recv, rs_send, rs_recv, move_send, move_recv,
     note_send, note_recv, out_sem,
 ):
@@ -58,24 +58,66 @@
     barrier = pltpu.get_barrier_semaphore()
     for k in range(1, n):
         pl.semaphore_signal(barrier, inc=1, device_id=(at_req(k), tp), device_id_type=MESH)
-    for k in range(1, t):
-        pl.semaphore_signal(barrier, inc=1, device_id=(req, at_tp(k)), device_id_type=MESH)
-    pl.semaphore_wait(barrier, n + t - 2)
-
-    def gather_copy(c, k, slot):
+
+    strides = [1 << j for j in range(t.bit_length() - 1)]
+
+    def flip(m):
+        place = tp
+        for b in strides:
+            if m & b:
+                place = place + b * (1 - 2 * lax.rem(tp // b, 2))
+        return place
+
+    for b in strides:
+        pl.semaphore_signal(barrier, inc=1, device_id=(req, flip(b)), device_id_type=MESH)
+    pl.semaphore_wait(barrier, n - 1 + len(strides))
+
+    def low(m):
+        return m & -m
+
+    def gather_copy(c, m, b):
+        slot = flip(m)
         return pltpu.make_async_remote_copy(
-            src_ref=hidden.at[pl.ds(c * crows, crows)],
+            src_ref=full.at[c, slot],
             dst_ref=full.at[c, slot],
-            send_sem=ag_send.at[c, k],
-            recv_sem=ag_recv.at[c, slot],
-            device_id=(req, at_tp(k)),
+            send_sem=ag_send.at[c, m | b],
+            recv_sem=ag_recv.at[c, m | b],
+            device_id=(req, flip(b)),
             device_id_type=MESH,
         )
 
+    def gather_start(c):
+        full[c, tp] = hidden[c * crows : (c + 1) * crows]
+        for b in reversed(strides):
+            gather_copy(c, 0, b).start()
+
+    def gather_wait(c, m):
+        slot = flip(m)
+        pltpu.make_async_remote_copy(
+            src_ref=full.at[c, slot],
+            dst_ref=full.at[c, slot],
+            send_sem=ag_send.at[c, m],
+            recv_sem=ag_recv.at[c, m],
+            device_id=(req, flip(low(m))),
+            device_id_type=MESH,
+        ).wait_recv()
+
+    passed_on = sorted((m for m in range(2, t) if low(m) > 1), key=low, reverse=True)
+
+    def gather_pass(c):
+        for m in passed_on:
+            gather_wait(c, m)
+            for b in reversed(strides):
+                if b < low(m):
+                    gather_copy(c, m, b).start()
+
+    def gather_end(c):
+        for m in range(1, t, 2):
+            gather_wait(c, m)
+
     for c in range(chunks):
-        for k in range(1, t):
-            gather_copy(c, k, tp).start()
-        full[c, tp] = hidden[c * crows : (c + 1) * crows]
+        gather_start(c)
+    gains = gain[...].reshape(1, t * width)
 
     positions = lax.broadcasted_iota(jnp.int32, (1, cache_len), 1)
 
@@ -111,9 +153,14 @@
     own = request_for(req)
     landed[0] = jnp.where(positions < lengths[own], kept[own], jnp.zeros((), BF16))
 
-    seen = lax.broadcasted_iota(jnp.int32, (rows, rows), 1)
-    line = lax.broadcasted_iota(jnp.int32, (rows, rows), 0)
-    reach = jnp.logical_or(seen == parent[...], seen == line).astype(F32).astype(BF16)
+    gather_pass(0)
+
+    seen = lax.broadcasted_iota(jnp.int32, (rows, rows), 0)
+    line = lax.broadcasted_iota(jnp.int32, (rows, rows), 1)
+    parent_row = jnp.concatenate(
+        [parent[r : r + 1, :] + r * tree for r in range(requests)], axis=1
+    )
+    reach = jnp.logical_or(seen == parent_row, seen == line).astype(F32).astype(BF16)
     covered = 1
     while covered < tree:
         reach = jnp.minimum(jnp.dot(reach, reach, preferred_element_type=F32), 1.0).astype(BF16)
@@ -122,27 +169,50 @@
         lax.rem(lax.broadcasted_iota(jnp.int32, (rows, tree), 0), tree)
         == lax.broadcasted_iota(jnp.int32, (rows, tree), 1)
     ).astype(F32).astype(BF16)
-    local = jnp.dot(reach, fold, preferred_element_type=F32)
+    local = lax.dot_general(reach, fold, (((0,), (0,)), ((), ())), preferred_element_type=F32)
     marks[...] = local.reshape(requests, tree, tree)
     depth[...] = (jnp.sum(local, axis=1, keepdims=True) - 1.0).reshape(requests, tree, 1)
 
+    for r in range(requests):
+        angles = (depth[r] + lengths[r].astype(F32)) * freq[...]
+        turns[0, r] = jnp.cos(angles)
+        turns[1, r] = jnp.sin(angles)
+
     for copy in loads:
         copy.wait()
 
-    def reduce_copy(c, k):
+    def reduce_copy(c, m):
         return pltpu.make_async_remote_copy(
-            src_ref=part.at[c, at_tp(k)],
-            dst_ref=terms.at[c, tp],
-            send_sem=rs_send.at[c, k],
-            recv_sem=rs_recv.at[c, tp],
-            device_id=(req, at_tp(k)),
+            src_ref=outgoing.at[c, m],
+            dst_ref=incoming.at[c, m],
+            send_sem=rs_send.at[c, m],
+            recv_sem=rs_recv.at[c, m],
+            device_id=(req, flip(low(m))),
             device_id_type=MESH,
         )
 
-    def chunk(c, carry):
-        for k in range(1, t):
-            peer = at_tp(k)
-            gather_copy(c, k, peer).wait_recv()
+    def reduce_sum(c, m):
+        value = part[c, flip(m)].astype(F32)
+        for b in strides:
+            if m == 0 or b < low(m):
+                reduce_copy(c, m | b).wait_recv()
+                value += incoming[c, m | b].astype(F32)
+        return value
+
+    def reduce_start(c):
+        for m in range(t - 1, 0, -2):
+            outgoing[c, m] = part[c, flip(m)]
+            reduce_copy(c, m).start()
+
+    def reduce_pass(c):
+        for m in sorted(passed_on, key=low):
+            outgoing[c, m] = reduce_sum(c, m).astype(BF16)
+            reduce_copy(c, m).start()
+
+    def chunk(c):
+        if c > 0:
+            gather_pass(c)
+        gather_end(c)
         spread = jnp.zeros((crows, 1), F32)
         for g in range(t):
             value = full[c, g].astype(F32)
@@ -150,17 +220,16 @@
         inverse = lax.rsqrt(spread / (t * width) + 1e-05)
         for g in range(t):
             value = full[c, g].astype(F32)
-            nrm[:, g * width : (g + 1) * width] = (value * inverse * gain[g : g + 1, :]).astype(BF16)
+            nrm[:, g * width : (g + 1) * width] = (value * inverse * gains[:, g * width : (g + 1) * width]).astype(BF16)
         normed = nrm[...]
         query = jnp.dot(normed, wq[...], preferred_element_type=F32)
         keyval = lax.dot_general(
             normed, wkv[...], (((1,), (1,)), ((), ())), preferred_element_type=F32
         )
-        place = jnp.concatenate(
-            [depth[c * per + i] + lengths[c * per + i].astype(F32) for i in range(per)], axis=0
-        )
-        angles = place * freq[...]
-        cosines, sines = jnp.cos(angles), jnp.sin(angles)
+        if c > 0:
+            reduce_pass(c - 1)
+        cosines = turns[0, c * per : (c + 1) * per].reshape(crows, HALF)
+        sines = turns[1, c * per : (c + 1) * per].reshape(crows, HALF)
 
         def turn(value):
             first, second = value[:, :HALF], value[:, HALF:]
@@ -212,32 +281,28 @@
                     ctx[i, :, h * HD : (h + 1) * HD] = value[j * tree : (j + 1) * tree]
             return inner
 
-        lax.fori_loop(0, per, attend, 0)
+        lax.fori_loop(0, per, attend, 0, unroll=2)
         rounded = ctx[...].reshape(crows, kv_local * GROUP * HD).astype(BF16)
         for g in range(t):
             part[c, g] = jnp.dot(
                 rounded, wo[:, g * width : (g + 1) * width], preferred_element_type=F32
             ).astype(BF16)
-        for k in range(1, t):
-            reduce_copy(c, k).start()
-        terms[c, tp] = part[c, tp]
-        return carry
-
-    lax.fori_loop(0, chunks, chunk, 0)
-
-    level = lax.broadcasted_iota(jnp.int32, (PAD, tree), 0)
-    token = lax.broadcasted_iota(jnp.int32, (PAD, tree), 1)
+
+    for c in range(chunks):
+        chunk(c)
+        reduce_start(c)
+
     level_c = lax.broadcasted_iota(jnp.int32, (PAD, cache_len), 0)
     place_c = lax.broadcasted_iota(jnp.int32, (PAD, cache_len), 1)
-    n_accept = accepted.shape[1]
+    n_accept = accepted.shape[0]
+    token = lax.broadcasted_iota(jnp.int32, (n_accept, tree), 1)
+    asked = lax.broadcasted_iota(jnp.int32, accepted.shape, 1)
 
     def write_note(k, target):
         r = request_for(at_req(k))
-        pick = jnp.zeros((PAD, tree), F32)
-        for m in range(n_accept):
-            hit = jnp.logical_and(level == m, token == accepted[r, m])
-            pick = jnp.where(hit, 1.0, pick)
-        pick = pick.astype(BF16)
+        path = jnp.sum(jnp.where(asked == r, accepted[...], 0), axis=1, keepdims=True)
+        pick = (token == path).astype(F32)
+        pick = jnp.concatenate([pick, jnp.zeros((PAD - n_accept, tree), F32)], axis=0).astype(BF16)
         spot = jnp.logical_and(place_c == level_c + lengths[r], level_c < n_accept)
         target[k, 0:PAD, :] = spot.astype(F32).astype(BF16)
         chosen = [
@@ -280,6 +345,7 @@
         out_copy(k).start()
 
     finish(0)
+    reduce_pass(chunks - 1)
 
     def receive(k, carry):
         move_copy(k).wait_recv()
@@ -289,30 +355,17 @@
 
     lax.fori_loop(1, n, receive, 0)
 
-    def close(c, carry):
-        for k in range(1, t):
-            peer = at_tp(k)
-            pltpu.make_async_remote_copy(
-                src_ref=part.at[c, peer],
-                dst_ref=terms.at[c, peer],
-                send_sem=rs_send.at[c, k],
-                recv_sem=rs_recv.at[c, peer],
-                device_id=(req, peer),
-                device_id_type=MESH,
-            ).wait_recv()
-        summed = terms[c, 0].astype(F32)
-        for g in range(1, t):
-            summed += terms[c, g].astype(F32)
-        where = pl.ds(pl.multiple_of(c * crows, 16), crows)
-        out_rows[where, :] = (hidden[where, :].astype(F32) + summed).astype(BF16)
-        return carry
-
-    lax.fori_loop(0, chunks, close, 0)
-
     for c in range(chunks):
-        for k in range(1, t):
-            gather_copy(c, k, tp).wait_send()
-            reduce_copy(c, k).wait_send()
+        where = slice(c * crows, (c + 1) * crows)
+        out_rows[where, :] = (reduce_sum(c, 0) + hidden[where, :].astype(F32)).astype(BF16)
+
+    for c in range(chunks):
+        for m in range(t):
+            for b in strides:
+                if m == 0 or b < low(m):
+                    gather_copy(c, m, b).wait_send()
+        for m in range(1, t):
+            reduce_copy(c, m).wait_send()
 
     def drain(k, carry):
         move_copy(k).wait_send()
@@ -322,6 +375,11 @@
 
     lax.fori_loop(1, n, drain, 0)
     out_copy(0).wait()
+
+
+def hand_over(rows, cache, out_rows, new_cache):
+    out_rows[...] = rows[...]
+    new_cache[...] = cache[...]
 
 
 def per_device(
@@ -341,7 +399,6 @@
     freq = jnp.asarray(
         (10000.0 ** (-2.0 * np.arange(HALF, dtype=np.float64) / HD)).astype(np.float32)
     ).reshape(1, HALF)
-    parent = (parents + tree * jnp.arange(requests, dtype=jnp.int32)[:, None]).reshape(rows, 1)
     smem = pl.BlockSpec(memory_space=pltpu.SMEM)
     vmem = pl.BlockSpec(memory_space=pltpu.VMEM)
     hbm = pl.BlockSpec(memory_space=pl.ANY)
@@ -352,7 +409,7 @@
             jax.ShapeDtypeStruct((rows, width), BF16),
             jax.ShapeDtypeStruct(kv_cache.shape, BF16),
         ),
-        in_specs=[smem] * 3 + [vmem] * 4 + [hbm] * 4,
+        in_specs=[smem] * 2 + [vmem] * 5 + [hbm] * 4,
         out_specs=(vmem, hbm),
         scratch_shapes=[
             pltpu.VMEM(w_query.shape, BF16),
@@ -372,6 +429,8 @@
             pltpu.VMEM((per, tree, q_width), F32),
             pltpu.VMEM((chunks, t, crows, width), BF16),
             pltpu.VMEM((chunks, t, crows, width), BF16),
+            pltpu.VMEM((chunks, t, crows, width), BF16),
+            pltpu.VMEM((2, requests, tree, HALF), F32),
             dma((3,)),
             dma((requests,)),
             dma((chunks, t)),
@@ -388,9 +447,23 @@
             collective_id=0, has_side_effects=True, vmem_limit_bytes=56 * 1024 * 1024
         ),
     )(
-        lengths, slot_of, accepted, hidden.reshape(rows, width), norm_gain.reshape(t, width),
-        freq, parent, w_query, w_keyval, w_out, kv_cache,
+        lengths, slot_of, accepted.T, hidden.reshape(rows, width), norm_gain,
+        freq, parents, w_query, w_keyval, w_out, kv_cache,
     )
+    rows_shape, cache_shape = out_rows.shape, new_cache.shape
+    rows_spec = pl.BlockSpec((2 * tree, width), lambda i: (i, 0))
+    cache_spec = pl.BlockSpec((2,) + cache_shape[1:], lambda i: (i, 0, 0))
+    out_rows, new_cache = pl.pallas_call(
+        hand_over,
+        out_shape=(
+            jax.ShapeDtypeStruct(rows_shape, BF16),
+            jax.ShapeDtypeStruct(cache_shape, BF16),
+        ),
+        grid=(requests // 2,),
+        in_specs=[rows_spec, cache_spec],
+        out_specs=(rows_spec, cache_spec),
+        compiler_params=pltpu.CompilerParams(vmem_limit_bytes=60 * 1024 * 1024),
+    )(out_rows, new_cache)
     return (out_rows.reshape(requests, tree, width), new_cache)
 
 

time: 60.2 us -> 62.5 us (1.038)
  Pallas kernels: 49.5 us -> 61.6 us
  local copies, waits for them, and re-layouts: 8.45 us -> 0 us
  other arithmetic: 0.76 us -> 0 us
    pallas_call x1, Pallas kernels: 49.5 us -> 57.5 us  [per_device(): pl.pallas_call(functools.partial(kernel, n, t, chunks, requests, tree), o...]
    unnamed x3 -> x0, local copies, waits for them, and re-layouts: 6.4 us -> none
    pallas_call x0 -> x1, Pallas kernels: none -> 4.11 us  [per_device(): pl.pallas_call(hand_over, out_shape=(jax.ShapeDtypeStruct(rows_shape, BF1...]
    reshape x2 -> x0, local copies, waits for them, and re-layouts: 2.05 us -> none  [the longest x1 1.31 us: per_device(): norm_gain.reshape(t, width)]
    add x1 -> x0, other arithmetic: 0.76 us -> none  [per_device(): parents + tree * jnp.arange(requests, dtype=jnp.int32)[:, None]]
where the time goes in v3:
time: 62.5 us; the launch traced here: 62.3 us
  Pallas kernels  61.6 us (99%)
  between operations  0.64 us (1%)
    pallas_call x1, Pallas kernels, per_device(): pl.pallas_call(functools.partial(kernel, n, t, chunks, requests, tree), o...  57.5 us
    pallas_call x1, Pallas kernels, per_device(): pl.pallas_call(hand_over, out_shape=(jax.ShapeDtypeStruct(rows_shape, BF1...  4.11 us

profile of v3, /device:TPU:0, one launch (start us, length us, event | category | flops | bytes accessed | tf_op | source)
XLA Modules:
  0.0 62.3 jit_solution(12992675985653681114)
XLA Ops:
  0.6 57.5 %shard_map.122 = (bf16[192,640]{1,0:T(8,128)(2,1)}, bf16[8,320,512]{2,1,0:T(8,128)(2,1)}) custom-call(s32[8]{0:T(128)} %lengths.1, s32[8]{0:T(128)} %slots.1, s32[4,8]{1,0:T(4,128)} %bitcast.4, bf16[192,640]{1,0:T(8,128)(2,1)} %bitcast.3, f32[2560]{0:T(1024)} %gain.1, f32[1,40]{1,0:T(1,128)} %constant.3.freq, s32[8,24]{1,0:T(8,128)} %parent.1, ...), custom_call_target="tpu_custom_call" | custom-call | tf_op jit(solution)/shard_map/pallas_call | solution.py:406
  58.2 4.1 %shard_map.123 = (bf16[192,640]{1,0:T(8,128)(2,1)}, bf16[8,320,512]{2,1,0:T(8,128)(2,1)}) custom-call(bf16[192,640]{1,0:T(8,128)(2,1)} %get-tuple-element.6.rows, bf16[8,320,512]{2,1,0:T(8,128)(2,1)} %get-tuple-element.7.cache), custom_call_target="tpu_custom_call" | custom-call | tf_op jit(solution)/shard_map/pallas_call | solution.py:456

commit v4 on v3

--- a/solution.py
+++ b/solution.py
@@ -18,6 +18,8 @@
 F32 = jnp.float32
 BF16 = jnp.bfloat16
 PAD = 16
+LANES = 128
+TOGETHER = 2
 
 
 def kernel(
@@ -122,10 +124,18 @@
     positions = lax.broadcasted_iota(jnp.int32, (1, cache_len), 1)
 
     def request_for(dest):
-        def look(r, found):
-            return jnp.where(slots[r] // requests == dest, r, found)
-
-        return lax.fori_loop(0, requests, look, jnp.int32(0))
+        first = dest * requests
+        found = jnp.int32(0)
+        for r in range(1, requests):
+            here = jnp.logical_and(slots[r] >= first, slots[r] < first + requests)
+            found = jnp.where(here, r, found)
+        return found
+
+    def kept_only(r):
+        live = jnp.where(positions < lengths[r], 1.0, 0.0)
+        live = jnp.broadcast_to(live, (PAD, cache_len)).astype(BF16)
+        value = kept[r]
+        return (value.reshape(-1, PAD, cache_len) * live[None]).reshape(value.shape)
 
     def wait_cache(r, carry):
         pltpu.make_async_copy(cache.at[r], kept.at[r], cache_sem.at[r]).wait()
@@ -145,13 +155,13 @@
 
     def move(k, carry):
         r = request_for(at_req(k))
-        stage[k] = jnp.where(positions < lengths[r], kept[r], jnp.zeros((), BF16))
+        stage[k] = kept_only(r)
         move_copy(k).start()
         return carry
 
     lax.fori_loop(1, n, move, 0)
     own = request_for(req)
-    landed[0] = jnp.where(positions < lengths[own], kept[own], jnp.zeros((), BF16))
+    landed[0] = kept_only(own)
 
     gather_pass(0)
 
@@ -166,11 +176,11 @@
         reach = jnp.minimum(jnp.dot(reach, reach, preferred_element_type=F32), 1.0).astype(BF16)
         covered *= 2
     fold = (
-        lax.rem(lax.broadcasted_iota(jnp.int32, (rows, tree), 0), tree)
-        == lax.broadcasted_iota(jnp.int32, (rows, tree), 1)
+        lax.rem(lax.broadcasted_iota(jnp.int32, (rows, LANES), 0), tree)
+        == lax.broadcasted_iota(jnp.int32, (rows, LANES), 1)
     ).astype(F32).astype(BF16)
     local = lax.dot_general(reach, fold, (((0,), (0,)), ((), ())), preferred_element_type=F32)
-    marks[...] = local.reshape(requests, tree, tree)
+    marks[...] = local.reshape(requests, tree, LANES)
     depth[...] = (jnp.sum(local, axis=1, keepdims=True) - 1.0).reshape(requests, tree, 1)
 
     for r in range(requests):
@@ -210,8 +220,6 @@
             reduce_copy(c, m).start()
 
     def chunk(c):
-        if c > 0:
-            gather_pass(c)
         gather_end(c)
         spread = jnp.zeros((crows, 1), F32)
         for g in range(t):
@@ -226,6 +234,8 @@
         keyval = lax.dot_general(
             normed, wkv[...], (((1,), (1,)), ((), ())), preferred_element_type=F32
         )
+        if c + 1 < chunks:
+            gather_pass(c + 1)
         if c > 0:
             reduce_pass(c - 1)
         cosines = turns[0, c * per : (c + 1) * per].reshape(crows, HALF)
@@ -238,7 +248,7 @@
             )
 
         for h in range(kv_local * GROUP):
-            value = turn(query[:, h * HD : (h + 1) * HD])
+            value = turn(query[:, h * HD : (h + 1) * HD]) * scale
             qs[h] = value.reshape(per, tree, HD)
         for i in range(2 * kv_local):
             value = keyval[:, i * HD : (i + 1) * HD]
@@ -247,47 +257,52 @@
             value = value.astype(BF16).astype(F32).reshape(per, tree, HD)
             kvs[pl.ds(c * per, per), i] = value
 
-        def attend(i, inner):
-            r = c * per + i
-            live = positions < lengths[r]
-            mask = marks[r] > 0.5
-            mask = jnp.concatenate([mask.astype(F32)] * GROUP, axis=0) > 0.5
-            for g in range(kv_local):
+        def attend(pair, inner):
+            jobs = [(pair * TOGETHER + u, g) for u in range(TOGETHER) for g in range(kv_local)]
+            scores = []
+            for i, g in jobs:
+                r = c * per + i
                 q = qs[g * GROUP : (g + 1) * GROUP, i].reshape(GROUP * tree, HD).astype(BF16)
-                low = g * 2 * HD
-                keys = kept[r, low : low + HD, :]
-                values = kept[r, low + HD : low + 2 * HD, :]
-                tree_keys = kvs[r, 2 * g].astype(BF16)
-                tree_values = kvs[r, 2 * g + 1].astype(BF16)
-                a = jnp.dot(q, keys, preferred_element_type=F32) * scale
+                tree_keys = jnp.concatenate([kvs[r, 2 * g], blank], axis=0).astype(BF16)
+                keys = kept[r, g * 2 * HD : g * 2 * HD + HD, :]
+                a = jnp.dot(q, keys, preferred_element_type=F32)
                 b = lax.dot_general(
                     q, tree_keys, (((1,), (1,)), ((), ())), preferred_element_type=F32
-                ) * scale
-                a = jnp.where(live, a, -1e30)
-                b = jnp.where(mask, b, -1e30)
-                top = jnp.maximum(
-                    jnp.max(a, axis=1, keepdims=True), jnp.max(b, axis=1, keepdims=True)
                 )
-                a, b = jnp.exp(a - top), jnp.exp(b - top)
-                total = jnp.sum(a, axis=1, keepdims=True) + jnp.sum(b, axis=1, keepdims=True)
-                inverse_total = 1.0 / total
-                a = (a * inverse_total).astype(BF16)
-                b = (b * inverse_total).astype(BF16)
+                scores.append((a, b))
+            weights = []
+            for (i, g), (a, b) in zip(jobs, scores):
+                r = c * per + i
+                mask = jnp.concatenate([marks[r]] * GROUP, axis=0) > 0.5
+                both = jnp.concatenate(
+                    [jnp.where(positions < lengths[r], a, -1e30), jnp.where(mask, b, -1e30)], axis=1
+                )
+                both = jnp.exp(both - jnp.max(both, axis=1, keepdims=True))
+                weights.append((both.astype(BF16), jnp.sum(both, axis=1, keepdims=True)))
+            results = []
+            for (i, g), (both, total) in zip(jobs, weights):
+                r = c * per + i
+                values = kept[r, g * 2 * HD + HD : (g + 1) * 2 * HD, :]
+                tree_values = jnp.concatenate([kvs[r, 2 * g + 1], blank], axis=0).astype(BF16)
                 value = lax.dot_general(
-                    a, values, (((1,), (1,)), ((), ())), preferred_element_type=F32
-                ) + jnp.dot(b, tree_values, preferred_element_type=F32)
+                    both[:, :cache_len], values, (((1,), (1,)), ((), ())),
+                    preferred_element_type=F32,
+                ) + jnp.dot(both[:, cache_len:], tree_values, preferred_element_type=F32)
+                results.append(value / total)
+            for (i, g), value in zip(jobs, results):
                 for j in range(GROUP):
                     h = g * GROUP + j
                     ctx[i, :, h * HD : (h + 1) * HD] = value[j * tree : (j + 1) * tree]
             return inner
 
-        lax.fori_loop(0, per, attend, 0, unroll=2)
+        lax.fori_loop(0, per // TOGETHER, attend, 0)
         rounded = ctx[...].reshape(crows, kv_local * GROUP * HD).astype(BF16)
         for g in range(t):
             part[c, g] = jnp.dot(
                 rounded, wo[:, g * width : (g + 1) * width], preferred_element_type=F32
             ).astype(BF16)
 
+    blank = jnp.zeros((LANES - tree, HD), F32)
     for c in range(chunks):
         chunk(c)
         reduce_start(c)
@@ -377,9 +392,19 @@
     out_copy(0).wait()
 
 
-def hand_over(rows, cache, out_rows, new_cache):
-    out_rows[...] = rows[...]
-    new_cache[...] = cache[...]
+def hand_over(rows, cache, out_rows, new_cache, rows_held, held, in_sem, out_sem):
+    count = cache.shape[0]
+    moves = [(cache.at[i], held.at[i], new_cache.at[i]) for i in range(count)]
+    moves.append((rows, rows_held, out_rows))
+    first = [pltpu.make_async_copy(m[0], m[1], in_sem.at[i]) for i, m in enumerate(moves)]
+    second = [pltpu.make_async_copy(m[1], m[2], out_sem.at[i]) for i, m in enumerate(moves)]
+    for copy in first:
+        copy.start()
+    for copy, after in zip(first, second):
+        copy.wait()
+        after.start()
+    for copy in second:
+        copy.wait()
 
 
 def per_device(
@@ -424,7 +449,7 @@
             pltpu.VMEM((crows, features), BF16),
             pltpu.VMEM((heads, per, tree, HD), F32),
             pltpu.VMEM((requests, kv_rows // HD, tree, HD), F32),
-            pltpu.VMEM((requests, tree, tree), F32),
+            pltpu.VMEM((requests, tree, LANES), F32),
             pltpu.VMEM((requests, tree, 1), F32),
             pltpu.VMEM((per, tree, q_width), F32),
             pltpu.VMEM((chunks, t, crows, width), BF16),
@@ -451,17 +476,20 @@
         freq, parents, w_query, w_keyval, w_out, kv_cache,
     )
     rows_shape, cache_shape = out_rows.shape, new_cache.shape
-    rows_spec = pl.BlockSpec((2 * tree, width), lambda i: (i, 0))
-    cache_spec = pl.BlockSpec((2,) + cache_shape[1:], lambda i: (i, 0, 0))
     out_rows, new_cache = pl.pallas_call(
         hand_over,
         out_shape=(
             jax.ShapeDtypeStruct(rows_shape, BF16),
             jax.ShapeDtypeStruct(cache_shape, BF16),
         ),
-        grid=(requests // 2,),
-        in_specs=[rows_spec, cache_spec],
-        out_specs=(rows_spec, cache_spec),
+        in_specs=[hbm, hbm],
+        out_specs=(hbm, hbm),
+        scratch_shapes=[
+            pltpu.VMEM(rows_shape, BF16),
+            pltpu.VMEM(cache_shape, BF16),
+            dma((cache_shape[0] + 1,)),
+            dma((cache_shape[0] + 1,)),
+        ],
         compiler_params=pltpu.CompilerParams(vmem_limit_bytes=60 * 1024 * 1024),
     )(out_rows, new_cache)
     return (out_rows.reshape(requests, tree, width), new_cache)

time: 62.5 us -> 53.3 us (0.85)
  Pallas kernels: 61.6 us -> 52.5 us
    pallas_call x1, Pallas kernels: 57.5 us -> 49.8 us  [per_device(): pl.pallas_call(functools.partial(kernel, n, t, chunks, requests, tree), o...]
    pallas_call x1, Pallas kernels: 4.11 us -> 2.68 us  [per_device(): pl.pallas_call(hand_over, out_shape=(jax.ShapeDtypeStruct(rows_shape, BF1...]
where the time goes in v4:
time: 53.3 us; the launch traced here: 53.1 us
  Pallas kernels  52.5 us (98%)
  between operations  0.64 us (1%)
    pallas_call x1, Pallas kernels, per_device(): pl.pallas_call(functools.partial(kernel, n, t, chunks, requests, tree), o...  49.8 us
    pallas_call x1, Pallas kernels, per_device(): pl.pallas_call(hand_over, out_shape=(jax.ShapeDtypeStruct(rows_shape, BF1...  2.68 us

profile of v4, /device:TPU:0, one launch (start us, length us, event | category | flops | bytes accessed | tf_op | source)
XLA Modules:
  0.0 53.1 jit_solution(688815100118788619)
XLA Ops:
  0.6 49.8 %shard_map.122 = (bf16[192,640]{1,0:T(8,128)(2,1)}, bf16[8,320,512]{2,1,0:T(8,128)(2,1)}) custom-call(s32[8]{0:T(128)} %lengths.1, s32[8]{0:T(128)} %slots.1, s32[4,8]{1,0:T(4,128)} %bitcast.4, bf16[192,640]{1,0:T(8,128)(2,1)} %bitcast.3, f32[2560]{0:T(1024)} %gain.1, f32[1,40]{1,0:T(1,128)} %constant.3.freq, s32[8,24]{1,0:T(8,128)} %parent.1, ...), custom_call_target="tpu_custom_call" | custom-call | tf_op jit(solution)/shard_map/pallas_call | solution.py:431
  50.5 2.7 %shard_map.123 = (bf16[192,640]{1,0:T(8,128)(2,1)}, bf16[8,320,512]{2,1,0:T(8,128)(2,1)}) custom-call(bf16[192,640]{1,0:T(8,128)(2,1)} %get-tuple-element.6.rows, bf16[8,320,512]{2,1,0:T(8,128)(2,1)} %get-tuple-element.7.cache), custom_call_target="tpu_custom_call" | custom-call | tf_op jit(solution)/shard_map/pallas_call | solution.py:479

commit v5 on v4

--- a/solution.py
+++ b/solution.py
@@ -72,6 +72,34 @@
 
     for b in strides:
         pl.semaphore_signal(barrier, inc=1, device_id=(req, flip(b)), device_id_type=MESH)
+    positions = lax.broadcasted_iota(jnp.int32, (1, cache_len), 1)
+
+    def request_for(dest):
+        first = dest * requests
+        found = jnp.int32(0)
+        for r in range(1, requests):
+            here = jnp.logical_and(slots[r] >= first, slots[r] < first + requests)
+            found = jnp.where(here, r, found)
+        return found
+
+    def kept_only(r):
+        live = jnp.where(positions < lengths[r], 1.0, 0.0)
+        live = jnp.broadcast_to(live, (PAD, cache_len)).astype(BF16)
+        value = kept[r]
+        return (value.reshape(-1, PAD, cache_len) * live[None]).reshape(value.shape)
+
+    def wait_cache(r, carry):
+        pltpu.make_async_copy(cache.at[r], kept.at[r], cache_sem.at[r]).wait()
+        return carry
+
+    lax.fori_loop(0, requests, wait_cache, 0)
+
+    def put(k, carry):
+        stage[k] = kept_only(request_for(at_req(k)))
+        return carry
+
+    lax.fori_loop(1, n, put, 0)
+
     pl.semaphore_wait(barrier, n - 1 + len(strides))
 
     def low(m):
@@ -121,28 +149,6 @@
         gather_start(c)
     gains = gain[...].reshape(1, t * width)
 
-    positions = lax.broadcasted_iota(jnp.int32, (1, cache_len), 1)
-
-    def request_for(dest):
-        first = dest * requests
-        found = jnp.int32(0)
-        for r in range(1, requests):
-            here = jnp.logical_and(slots[r] >= first, slots[r] < first + requests)
-            found = jnp.where(here, r, found)
-        return found
-
-    def kept_only(r):
-        live = jnp.where(positions < lengths[r], 1.0, 0.0)
-        live = jnp.broadcast_to(live, (PAD, cache_len)).astype(BF16)
-        value = kept[r]
-        return (value.reshape(-1, PAD, cache_len) * live[None]).reshape(value.shape)
-
-    def wait_cache(r, carry):
-        pltpu.make_async_copy(cache.at[r], kept.at[r], cache_sem.at[r]).wait()
-        return carry
-
-    lax.fori_loop(0, requests, wait_cache, 0)
-
     def move_copy(k):
         return pltpu.make_async_remote_copy(
             src_ref=stage.at[k],
@@ -154,16 +160,11 @@
         )
 
     def move(k, carry):
-        r = request_for(at_req(k))
-        stage[k] = kept_only(r)
         move_copy(k).start()
         return carry
 
     lax.fori_loop(1, n, move, 0)
-    own = request_for(req)
-    landed[0] = kept_only(own)
-
-    gather_pass(0)
+    landed[0] = kept_only(request_for(req))
 
     seen = lax.broadcasted_iota(jnp.int32, (rows, rows), 0)
     line = lax.broadcasted_iota(jnp.int32, (rows, rows), 1)
@@ -182,6 +183,8 @@
     local = lax.dot_general(reach, fold, (((0,), (0,)), ((), ())), preferred_element_type=F32)
     marks[...] = local.reshape(requests, tree, LANES)
     depth[...] = (jnp.sum(local, axis=1, keepdims=True) - 1.0).reshape(requests, tree, 1)
+
+    gather_pass(0)
 
     for r in range(requests):
         angles = (depth[r] + lengths[r].astype(F32)) * freq[...]

time: 53.3 us -> 53.3 us (level)
  no operation moved by 1% of the time
where the time goes in v5:
time: 53.3 us; the launch traced here: 53.1 us
  Pallas kernels  52.5 us (98%)
  between operations  0.64 us (1%)
    pallas_call x1, Pallas kernels, per_device(): pl.pallas_call(functools.partial(kernel, n, t, chunks, requests, tree), o...  49.8 us
    pallas_call x1, Pallas kernels, per_device(): pl.pallas_call(hand_over, out_shape=(jax.ShapeDtypeStruct(rows_shape, BF1...  2.68 us

profile of v5, /device:TPU:0, one launch (start us, length us, event | category | flops | bytes accessed | tf_op | source)
XLA Modules:
  0.0 53.1 jit_solution(4949278882400737235)
XLA Ops:
  0.6 49.8 %shard_map.122 = (bf16[192,640]{1,0:T(8,128)(2,1)}, bf16[8,320,512]{2,1,0:T(8,128)(2,1)}) custom-call(s32[8]{0:T(128)} %lengths.1, s32[8]{0:T(128)} %slots.1, s32[4,8]{1,0:T(4,128)} %bitcast.4, bf16[192,640]{1,0:T(8,128)(2,1)} %bitcast.3, f32[2560]{0:T(1024)} %gain.1, f32[1,40]{1,0:T(1,128)} %constant.3.freq, s32[8,24]{1,0:T(8,128)} %parent.1, ...), custom_call_target="tpu_custom_call" | custom-call | tf_op jit(solution)/shard_map/pallas_call | solution.py:434
  50.4 2.7 %shard_map.123 = (bf16[192,640]{1,0:T(8,128)(2,1)}, bf16[8,320,512]{2,1,0:T(8,128)(2,1)}) custom-call(bf16[192,640]{1,0:T(8,128)(2,1)} %get-tuple-element.6.rows, bf16[8,320,512]{2,1,0:T(8,128)(2,1)} %get-tuple-element.7.cache), custom_call_target="tpu_custom_call" | custom-call | tf_op jit(solution)/shard_map/pallas_call | solution.py:482

commit v6 on v5

--- a/solution.py
+++ b/solution.py
@@ -140,13 +140,14 @@
             for b in reversed(strides):
                 if b < low(m):
                     gather_copy(c, m, b).start()
+        if c + 1 < chunks:
+            gather_start(c + 1)
 
     def gather_end(c):
         for m in range(1, t, 2):
             gather_wait(c, m)
 
-    for c in range(chunks):
-        gather_start(c)
+    gather_start(0)
     gains = gain[...].reshape(1, t * width)
 
     def move_copy(k):
@@ -213,11 +214,13 @@
         return value
 
     def reduce_start(c):
-        for m in range(t - 1, 0, -2):
+        for m in range(t - 1, 1, -2):
             outgoing[c, m] = part[c, flip(m)]
             reduce_copy(c, m).start()
 
     def reduce_pass(c):
+        outgoing[c, 1] = part[c, flip(1)]
+        reduce_copy(c, 1).start()
         for m in sorted(passed_on, key=low):
             outgoing[c, m] = reduce_sum(c, m).astype(BF16)
             reduce_copy(c, m).start()

time: 53.3 us -> 50 us (0.938)
  Pallas kernels: 52.5 us -> 49.1 us
    pallas_call x1, Pallas kernels: 49.8 us -> 46.5 us  [per_device(): pl.pallas_call(functools.partial(kernel, n, t, chunks, requests, tree), o...]
where the time goes in v6:
time: 50 us; the launch traced here: 49.8 us
  Pallas kernels  49.1 us (98%)
  between operations  0.64 us (1%)
    pallas_call x1, Pallas kernels, per_device(): pl.pallas_call(functools.partial(kernel, n, t, chunks, requests, tree), o...  46.5 us
    pallas_call x1, Pallas kernels, per_device(): pl.pallas_call(hand_over, out_shape=(jax.ShapeDtypeStruct(rows_shape, BF1...  2.68 us

profile of v6, /device:TPU:0, one launch (start us, length us, event | category | flops | bytes accessed | tf_op | source)
XLA Modules:
  0.0 49.8 jit_solution(17774866345696494499)
XLA Ops:
  0.6 46.5 %shard_map.122 = (bf16[192,640]{1,0:T(8,128)(2,1)}, bf16[8,320,512]{2,1,0:T(8,128)(2,1)}) custom-call(s32[8]{0:T(128)} %lengths.1, s32[8]{0:T(128)} %slots.1, s32[4,8]{1,0:T(4,128)} %bitcast.4, bf16[192,640]{1,0:T(8,128)(2,1)} %bitcast.3, f32[2560]{0:T(1024)} %gain.1, f32[1,40]{1,0:T(1,128)} %constant.3.freq, s32[8,24]{1,0:T(8,128)} %parent.1, ...), custom_call_target="tpu_custom_call" | custom-call | tf_op jit(solution)/shard_map/pallas_call | solution.py:437
  47.1 2.7 %shard_map.123 = (bf16[192,640]{1,0:T(8,128)(2,1)}, bf16[8,320,512]{2,1,0:T(8,128)(2,1)}) custom-call(bf16[192,640]{1,0:T(8,128)(2,1)} %get-tuple-element.6.rows, bf16[8,320,512]{2,1,0:T(8,128)(2,1)} %get-tuple-element.7.cache), custom_call_target="tpu_custom_call" | custom-call | tf_op jit(solution)/shard_map/pallas_call | solution.py:485
